TPU v7x, 32 devices: a whole 2x2x4 slice. The times are simulated.
32 devices in a mesh: dp: 2 (over x), ctx: 4 (over z), tensor: 4 (over y, core).
Axes of the slice: x: 2, y: 2, z: 4, core: 2. Of those that a mesh axis runs over, the one named last changes fastest.
Arguments:
- hidden_in: bfloat16 [4, 1024, 768], P('dp', 'ctx'), may hold values from -6 to 6
- cotangent: bfloat16 [4, 1024, 768], P('dp', 'ctx'), may hold values from -6 to 6
- segment_ids: int32 [4, 1024], P('dp'), may hold values from 0 to 2, as said below
- qkv_weight: float32 [3, 768, 768], P(None, ('dp', 'ctx'), 'tensor'), may hold values from -0.21875 to 0.21875
- qkv_first: float32 [3, 768, 768], P(None, ('dp', 'ctx'), 'tensor'), may hold values from -16 to 16
- qkv_second: float32 [3, 768, 768], P(None, ('dp', 'ctx'), 'tensor'), may hold values from 0.53248 to 2.12992
- out_weight: float32 [768, 768], P('tensor', ('dp', 'ctx')), may hold values from -0.875 to 0.875
- out_first: float32 [768, 768], P('tensor', ('dp', 'ctx')), may hold values from -16 to 16
- out_second: float32 [768, 768], P('tensor', ('dp', 'ctx')), may hold values from 0.6144 to 2.4576
- up_weight: float32 [768, 3072], P(('dp', 'ctx'), 'tensor'), may hold values from -0.21875 to 0.21875
- up_first: float32 [768, 3072], P(('dp', 'ctx'), 'tensor'), may hold values from -16 to 16
- up_second: float32 [768, 3072], P(('dp', 'ctx'), 'tensor'), may hold values from 0.53248 to 2.12992
- down_weight: float32 [3072, 768], P('tensor', ('dp', 'ctx')), may hold values from -0.109375 to 0.109375
- down_first: float32 [3072, 768], P('tensor', ('dp', 'ctx')), may hold values from -28 to 28
- down_second: float32 [3072, 768], P('tensor', ('dp', 'ctx')), may hold values from 1.72032 to 6.9632
- vectors: float32 [12, 768], P(None, ('dp', 'ctx')), may hold values from -1.75 to 1.75
- vectors_first: float32 [12, 768], P(None, ('dp', 'ctx')), may hold values from -40 to 40
- vectors_second: float32 [12, 768], P(None, ('dp', 'ctx')), may hold values from 4.096 to 16.384
Outputs:
- block_out: bfloat16 [4, 1024, 768], P('dp', ('ctx', 'tensor'))
- input_grad: float32 [4, 1024, 768], P('dp', ('ctx', 'tensor'))
- qkv_new: float32 [3, 768, 768], P(None, ('dp', 'ctx'), 'tensor')
- qkv_first_new: float32 [3, 768, 768], P(None, ('dp', 'ctx'), 'tensor')
- qkv_second_new: float32 [3, 768, 768], P(None, ('dp', 'ctx'), 'tensor')
- out_new: float32 [768, 768], P('tensor', ('dp', 'ctx'))
- out_first_new: float32 [768, 768], P('tensor', ('dp', 'ctx'))
- out_second_new: float32 [768, 768], P('tensor', ('dp', 'ctx'))
- up_new: float32 [768, 3072], P(('dp', 'ctx'), 'tensor')
- up_first_new: float32 [768, 3072], P(('dp', 'ctx'), 'tensor')
- up_second_new: float32 [768, 3072], P(('dp', 'ctx'), 'tensor')
- down_new: float32 [3072, 768], P('tensor', ('dp', 'ctx'))
- down_first_new: float32 [3072, 768], P('tensor', ('dp', 'ctx'))
- down_second_new: float32 [3072, 768], P('tensor', ('dp', 'ctx'))
- vectors_new: float32 [12, 768], P(None, ('dp', 'ctx'))
- vectors_first_new: float32 [12, 768], P(None, ('dp', 'ctx'))
- vectors_second_new: float32 [12, 768], P(None, ('dp', 'ctx'))
Inputs may be any that keep to these rules, and one draw needn't show every extreme that they name: `segment_ids`: each sequence holds three documents numbered 0, 1, 2 in order; document 1 starts at a token index from 64 to 128, and document 2 starts at a token index from 896 to 960.
All inputs are finite; a program needn't handle non-finite values.
Results may differ from a plain program's by a relative error of at most 0.009.
The roundings to bfloat16 on the way count: a program that leaves them out, or rounds other values in their place, can miss the bound.
Values may be sent and summed in bfloat16 or wider, within the bound.
A program may use at most 128 MiB of HBM per device.

v0:
```python
import jax
import jax.numpy as jnp
from jax import lax
from jax.sharding import PartitionSpec as P

HD = 64
STEP = 10


norm_eps = 1e-05
beta_first = 0.9
beta_second = 0.999
adam_eps = 1e-08
weight_decay = 0.01
rate_qkv = 0.05
rate_out = 0.2
rate_up = 0.05
rate_down = 0.025
rate_vectors = 0.3


def normed(values, gain, shift):
    centre = values - jnp.mean(values, axis=-1, keepdims=True)
    spread = jnp.mean(centre * centre, axis=-1, keepdims=True)
    return centre * lax.rsqrt(spread + norm_eps) * gain + shift


def adamw(weight, first, second, grad, rate, decay):
    first_new = beta_first * first + (1.0 - beta_first) * grad
    second_new = beta_second * second + (1.0 - beta_second) * grad * grad
    fix_first = 1.0 - beta_first**STEP
    fix_second = 1.0 - beta_second**STEP
    update = first_new / fix_first / (jnp.sqrt(second_new / fix_second) + adam_eps)
    return (weight - rate * (update + decay * weight), first_new, second_new)


def fetch_rows(masters):
    return (
        lax.all_gather(masters[0].astype(jnp.bfloat16), ("dp", "ctx"), axis=1, tiled=True),
        lax.all_gather(masters[1].astype(jnp.bfloat16), ("dp", "ctx"), axis=1, tiled=True),
        lax.all_gather(masters[2].astype(jnp.bfloat16), ("dp", "ctx"), axis=0, tiled=True),
        lax.all_gather(masters[3].astype(jnp.bfloat16), ("dp", "ctx"), axis=1, tiled=True),
        lax.all_gather(masters[4].astype(jnp.bfloat16), ("dp", "ctx"), axis=1, tiled=True),
    )


def gather_keys(local_kv):
    return lax.all_gather(local_kv, "ctx", axis=0, tiled=True)


def share_rows(values):
    part = values.shape[0] // lax.axis_size("tensor")
    return lax.dynamic_slice_in_dim(values, lax.axis_index("tensor") * part, part, 0)


def allowed_pairs(segment, tokens):
    ctx_index = lax.axis_index("ctx")
    key_places = jnp.arange(segment.shape[0], dtype=jnp.int32)
    query_places = ctx_index * tokens + jnp.arange(tokens, dtype=jnp.int32)
    query_segment = lax.dynamic_slice_in_dim(segment, ctx_index * tokens, tokens)
    return (query_places[:, None] >= key_places[None, :]) & (
        query_segment[:, None] == segment[None, :]
    )


def head_scores(query, all_kv, allowed, local_width):
    tokens = query.shape[0]
    heads_here = local_width // HD
    query_heads = query.reshape(tokens, heads_here, HD)
    key_heads = all_kv[:, :local_width].reshape(all_kv.shape[0], heads_here, HD)
    scores = jnp.einsum(
        "qhd,khd->hqk", query_heads, key_heads, preferred_element_type=jnp.float32
    ) * HD ** (-0.5)
    return jnp.where(allowed[None], scores, -1e30)


def forward_pass(inputs, segment, weights):
    proj_all, out_full, up_full, down_full, table_low = weights
    table = table_low.astype(jnp.float32)
    tensor_index = lax.axis_index("tensor")
    local_width = proj_all.shape[2]
    unit_width = up_full.shape[1]
    tokens = inputs.shape[0]
    heads_here = local_width // HD
    first_norm = normed(inputs, table[0], table[1]).astype(jnp.bfloat16)
    projected = jnp.einsum("td,kde->kte", first_norm, proj_all, preferred_element_type=jnp.float32)
    query_bias = lax.dynamic_slice_in_dim(table[2], tensor_index * local_width, local_width)
    value_bias = lax.dynamic_slice_in_dim(table[3], tensor_index * local_width, local_width)
    query = (projected[0] + query_bias).astype(jnp.bfloat16)
    local_kv = jnp.concatenate([projected[1], projected[2] + value_bias], axis=1).astype(
        jnp.bfloat16
    )
    all_kv = gather_keys(local_kv)
    allowed = allowed_pairs(segment, tokens)
    scores = head_scores(query, all_kv, allowed, local_width)
    highest_score = jnp.max(scores, axis=-1, keepdims=True)
    weights_exp = jnp.exp(scores - highest_score)
    totals = jnp.sum(weights_exp, axis=-1, keepdims=True)
    probs_full = weights_exp / totals
    log_total = highest_score + jnp.log(totals)
    value_heads = all_kv[:, local_width:].reshape(all_kv.shape[0], heads_here, HD)
    mixed = jnp.einsum(
        "hqk,khd->qhd",
        probs_full.astype(jnp.bfloat16),
        value_heads,
        preferred_element_type=jnp.float32,
    )
    mixed = mixed.reshape(tokens, local_width).astype(jnp.bfloat16)
    attn_part = jnp.dot(mixed, out_full, preferred_element_type=jnp.float32)
    middle = inputs + lax.psum(attn_part, "tensor") + table[4]
    second_norm = normed(middle, table[5], table[6]).astype(jnp.bfloat16)
    unit_bias = lax.dynamic_slice_in_dim(
        table[8:].reshape(-1), tensor_index * unit_width, unit_width
    )
    hidden = jnp.dot(second_norm, up_full, preferred_element_type=jnp.float32) + unit_bias
    active = jax.nn.gelu(hidden).astype(jnp.bfloat16)
    down_part = jnp.dot(active, down_full, preferred_element_type=jnp.float32)
    result = share_rows(middle + lax.psum(down_part, "tensor") + table[7])
    saved = (
        first_norm,
        query,
        local_kv,
        all_kv,
        allowed,
        log_total,
        mixed,
        middle,
        second_norm,
        hidden,
        active,
    )
    return (result, saved)


def backward_pass(back, inputs, weights, saved, all_kv):
    proj_all, out_full, up_full, down_full, table_low = weights
    table = table_low.astype(jnp.float32)
    (
        first_norm,
        query,
        local_kv,
        kept_kv,
        allowed,
        log_total,
        mixed,
        middle,
        second_norm,
        hidden,
        active,
    ) = saved
    tensor_index = lax.axis_index("tensor")
    local_width = proj_all.shape[2]
    unit_width = up_full.shape[1]
    model_width = table.shape[1]
    table_rows = table.shape[0]
    tokens = inputs.shape[0]
    heads_here = local_width // HD
    back_low = back.astype(jnp.bfloat16)
    grad_down = jnp.einsum("tf,td->fd", active, back_low, preferred_element_type=jnp.float32)
    unit_grad = jnp.einsum("td,fd->tf", back_low, down_full, preferred_element_type=jnp.float32)
    gelu_value, gelu_pull = jax.vjp(jax.nn.gelu, hidden)
    hidden_grad = gelu_pull(unit_grad)[0]
    hidden_low = hidden_grad.astype(jnp.bfloat16)
    grad_up = jnp.einsum("td,tf->df", second_norm, hidden_low, preferred_element_type=jnp.float32)
    second_part = jnp.einsum("tf,df->td", hidden_low, up_full, preferred_element_type=jnp.float32)
    second_grad = lax.psum(second_part, "tensor")
    norm_value, second_pull = jax.vjp(normed, middle, table[5], table[6])
    middle_from_norm, gain_second, shift_second = second_pull(second_grad)
    middle_grad = back + middle_from_norm
    middle_low = middle_grad.astype(jnp.bfloat16)
    grad_out = jnp.einsum("te,td->ed", mixed, middle_low, preferred_element_type=jnp.float32)
    mixed_grad = jnp.einsum(
        "td,ed->te", middle_low, out_full, preferred_element_type=jnp.float32
    ).astype(jnp.bfloat16)
    scores = head_scores(query, all_kv, allowed, local_width)
    probs_full = jnp.exp(scores - log_total)
    key_heads = all_kv[:, :local_width].reshape(all_kv.shape[0], heads_here, HD)
    value_heads = all_kv[:, local_width:].reshape(all_kv.shape[0], heads_here, HD)
    mixed_heads = mixed_grad.reshape(tokens, heads_here, HD)
    query_heads = query.reshape(tokens, heads_here, HD)
    prob_grad = jnp.einsum(
        "qhd,khd->hqk", mixed_heads, value_heads, preferred_element_type=jnp.float32
    )
    row_delta = jnp.sum(prob_grad * probs_full, axis=-1, keepdims=True)
    score_grad = (probs_full * (prob_grad - row_delta) * HD ** (-0.5)).astype(jnp.bfloat16)
    probs_low = probs_full.astype(jnp.bfloat16)
    query_grad = jnp.einsum(
        "hqk,khd->qhd", score_grad, key_heads, preferred_element_type=jnp.float32
    ).reshape(tokens, local_width)
    key_part = jnp.einsum(
        "hqk,qhd->khd", score_grad, query_heads, preferred_element_type=jnp.float32
    )
    value_part = jnp.einsum(
        "hqk,qhd->khd", probs_low, mixed_heads, preferred_element_type=jnp.float32
    )
    kv_grad = lax.psum_scatter(
        jnp.concatenate(
            [
                key_part.reshape(lax.axis_size("ctx") * tokens, local_width),
                value_part.reshape(lax.axis_size("ctx") * tokens, local_width),
            ],
            axis=1,
        ),
        "ctx",
        scatter_dimension=0,
        tiled=True,
    )
    key_grad = kv_grad[:, :local_width]
    value_grad = kv_grad[:, local_width:]
    stacked = jnp.stack([query_grad, key_grad, value_grad]).astype(jnp.bfloat16)
    grad_qkv = jnp.einsum("td,kte->kde", first_norm, stacked, preferred_element_type=jnp.float32)
    first_part = jnp.einsum("kte,kde->td", stacked, proj_all, preferred_element_type=jnp.float32)
    owned = jnp.zeros((table_rows * model_width,), jnp.float32)
    owned = lax.dynamic_update_slice(
        owned, jnp.sum(query_grad, axis=0), (2 * model_width + tensor_index * local_width,)
    )
    owned = lax.dynamic_update_slice(
        owned, jnp.sum(value_grad, axis=0), (3 * model_width + tensor_index * local_width,)
    )
    owned = lax.dynamic_update_slice(
        owned, jnp.sum(hidden_grad, axis=0), (8 * model_width + tensor_index * unit_width,)
    )
    late_rows = jnp.stack(
        [jnp.sum(middle_grad, axis=0), gain_second, shift_second, jnp.sum(back, axis=0)]
    )
    late_flat = jnp.concatenate(
        [
            jnp.zeros((4 * model_width,), jnp.float32),
            late_rows.reshape(-1),
            jnp.zeros(((table_rows - 8) * model_width,), jnp.float32),
        ]
    )
    first_grad, owned_sum = lax.psum((first_part, owned), "tensor")
    first_value, first_pull = jax.vjp(normed, inputs, table[0], table[1])
    input_from_norm, gain_first, shift_first = first_pull(first_grad)
    input_grad = share_rows(middle_grad + input_from_norm)
    early_flat = jnp.concatenate(
        [gain_first, shift_first, jnp.zeros(((table_rows - 2) * model_width,), jnp.float32)]
    )
    grad_table = (early_flat + late_flat + owned_sum).reshape(table.shape)
    return (input_grad, (grad_qkv, grad_out, grad_up, grad_down, grad_table))


def on_device(
    hidden_in,
    cotangent,
    segment_ids,
    qkv_weight,
    qkv_first,
    qkv_second,
    out_weight,
    out_first,
    out_second,
    up_weight,
    up_first,
    up_second,
    down_weight,
    down_first,
    down_second,
    vectors,
    vectors_first,
    vectors_second,
):
    masters = (qkv_weight, out_weight, up_weight, down_weight, vectors)
    results = []
    input_grads = []
    totals = None
    for batch in range(hidden_in.shape[0]):
        forward_weights = fetch_rows(masters)
        inputs = hidden_in[batch].astype(jnp.float32)
        result, saved = forward_pass(inputs, segment_ids[batch], forward_weights)
        results.append(result.astype(jnp.bfloat16))
        backward_weights = fetch_rows(masters)
        key_values = saved[3]
        back = cotangent[batch].astype(jnp.float32)
        input_grad, grads = backward_pass(back, inputs, backward_weights, saved, key_values)
        input_grads.append(input_grad)
        if totals is None:
            totals = grads
        else:
            totals = jax.tree.map(lambda left, right: left + right, totals, grads)
    summed = (
        lax.psum_scatter(totals[0], ("dp", "ctx"), scatter_dimension=1, tiled=True),
        lax.psum_scatter(totals[1], ("dp", "ctx"), scatter_dimension=1, tiled=True),
        lax.psum_scatter(totals[2], ("dp", "ctx"), scatter_dimension=0, tiled=True),
        lax.psum_scatter(totals[3], ("dp", "ctx"), scatter_dimension=1, tiled=True),
        lax.psum_scatter(totals[4], ("dp", "ctx"), scatter_dimension=1, tiled=True),
    )
    qkv_new, qkv_first_new, qkv_second_new = adamw(
        qkv_weight, qkv_first, qkv_second, summed[0], rate_qkv, weight_decay
    )
    out_new, out_first_new, out_second_new = adamw(
        out_weight, out_first, out_second, summed[1], rate_out, weight_decay
    )
    up_new, up_first_new, up_second_new = adamw(
        up_weight, up_first, up_second, summed[2], rate_up, weight_decay
    )
    down_new, down_first_new, down_second_new = adamw(
        down_weight, down_first, down_second, summed[3], rate_down, weight_decay
    )
    vectors_new, vectors_first_new, vectors_second_new = adamw(
        vectors, vectors_first, vectors_second, summed[4], rate_vectors, 0.0
    )
    return (
        jnp.stack(results),
        jnp.stack(input_grads),
        qkv_new,
        qkv_first_new,
        qkv_second_new,
        out_new,
        out_first_new,
        out_second_new,
        up_new,
        up_first_new,
        up_second_new,
        down_new,
        down_first_new,
        down_second_new,
        vectors_new,
        vectors_first_new,
        vectors_second_new,
    )


def solution(mesh):
    return jax.shard_map(
        on_device,
        mesh=mesh,
        in_specs=(
            P("dp", "ctx", None),
            P("dp", "ctx", None),
            P("dp", None),
            P(None, ("dp", "ctx"), "tensor"),
            P(None, ("dp", "ctx"), "tensor"),
            P(None, ("dp", "ctx"), "tensor"),
            P("tensor", ("dp", "ctx")),
            P("tensor", ("dp", "ctx")),
            P("tensor", ("dp", "ctx")),
            P(("dp", "ctx"), "tensor"),
            P(("dp", "ctx"), "tensor"),
            P(("dp", "ctx"), "tensor"),
            P("tensor", ("dp", "ctx")),
            P("tensor", ("dp", "ctx")),
            P("tensor", ("dp", "ctx")),
            P(None, ("dp", "ctx")),
            P(None, ("dp", "ctx")),
            P(None, ("dp", "ctx")),
        ),
        out_specs=(
            P("dp", ("ctx", "tensor"), None),
            P("dp", ("ctx", "tensor"), None),
            P(None, ("dp", "ctx"), "tensor"),
            P(None, ("dp", "ctx"), "tensor"),
            P(None, ("dp", "ctx"), "tensor"),
            P("tensor", ("dp", "ctx")),
            P("tensor", ("dp", "ctx")),
            P("tensor", ("dp", "ctx")),
            P(("dp", "ctx"), "tensor"),
            P(("dp", "ctx"), "tensor"),
            P(("dp", "ctx"), "tensor"),
            P("tensor", ("dp", "ctx")),
            P("tensor", ("dp", "ctx")),
            P("tensor", ("dp", "ctx")),
            P(None, ("dp", "ctx")),
            P(None, ("dp", "ctx")),
            P(None, ("dp", "ctx")),
        ),
        check_vma=False,
    )
```

profile of v0, /device:TPU:0, one launch (start us, length us, event | category | flops | bytes accessed | tf_op | source)
XLA Modules:
  0.0 773.6 jit_solution(7542640517843470665)
XLA Ops:
  10.1 32.1 %all-gather = bf16[8,96,12]{1,2,0:T(8,128)(2,1)S(1)} all-gather(bf16[1,96,12]{1,2,0:T(8,128)(2,1)S(1)} %convert_bitcast_fusion.2), channel_id=1, replica_groups=mesh['dp'=2,'ctx'=4,'tensor'=4] {'dp','ctx'}, dimensions={0}, use_global_device_ids=true | all-gather | bytes 20736 | tf_op jit(solution)/shard_map/all_gather | solution.py:43
  44.1 39.8 %all_gather.15 = bf16[3,768,192]{2,0,1:T(4,128)(2,1)S(1)} all-gather(bf16[3,96,192]{2,0,1:T(4,128)(2,1)S(1)} %copy.71), channel_id=1, replica_groups=mesh['dp'=2,'ctx'=4,'tensor'=4] {'dp','ctx'}, dimensions={1}, use_global_device_ids=true | all-gather | bytes 995328 | tf_op jit(solution)/shard_map/all_gather | solution.py:39
  88.2 16.2 %all_gather.16 = bf16[1024,384]{0,1:T(8,128)(2,1)S(1)} all-gather(bf16[256,384]{0,1:T(8,128)(2,1)S(1)} %pad_maximum_fusion.5), channel_id=1, replica_groups=mesh['dp'=2,'ctx'=4,'tensor'=4] {'ctx'}, dimensions={0}, use_global_device_ids=true | all-gather | bytes 983040 | tf_op jit(solution)/shard_map/all_gather | solution.py:48
  105.6 31.9 %all_gather.17 = bf16[192,768]{0,1:T(8,128)(2,1)S(1)} all-gather(bf16[192,96]{0,1:T(8,128)(2,1)S(1)} %copy.73), channel_id=1, replica_groups=mesh['dp'=2,'ctx'=4,'tensor'=4] {'dp','ctx'}, dimensions={1}, use_global_device_ids=true | all-gather | bytes 331776 | tf_op jit(solution)/shard_map/all_gather | solution.py:40
  137.5 15.8 %all_gather.20 = bf16[1024,384]{0,1:T(8,128)(2,1)S(1)} all-gather(bf16[256,384]{0,1:T(8,128)(2,1)S(1)} %pad_maximum_fusion.6), channel_id=1, replica_groups=mesh['dp'=2,'ctx'=4,'tensor'=4] {'ctx'}, dimensions={0}, use_global_device_ids=true | all-gather | bytes 983040 | tf_op jit(solution)/shard_map/all_gather | solution.py:48
  170.3 37.4 %all-reduce.15.cloned.1.call-done = (f32[256,768]{1,0:T(8,128)}, f32[256,768]{1,0:T(8,128)}) async-done(((f32[256,768]{1,0:T(8,128)}, f32[256,768]{1,0:T(8,128)}), (f32[256,768]{1,0:T(8,128)}, f32[256,768]{1,0:T(8,128)})) %all-reduce.15.cloned.1.call-update) | async-done | bytes 1572880 | tf_op jit(solution)/shard_map/psum | solution.py:110
  219.4 69.3 %reduce-scatter.20.cloned.1.call-done = f32[768,96]{0,1:T(8,128)} async-done(((f32[768,768]{0,1:T(8,128)}), f32[768,96]{0,1:T(8,128)}) %reduce-scatter.20.cloned.1.call-update) | async-done | bytes 294928 | tf_op jit(solution)/shard_map/reduce_scatter | solution.py:286
  291.2 40.7 %all-gather.6.cloned.1.call-done = bf16[768,768]{0,1:T(8,128)(2,1)} async-done(((bf16[768,96]{0,1:T(8,128)(2,1)}), bf16[768,768]{0,1:T(8,128)(2,1)}) %all-gather.6.cloned.1.call-update) | async-done | bytes 1179664 | tf_op jit(solution)/shard_map/all_gather | solution.py:42
  340.6 40.3 %all-reduce.13.cloned.1.call-done = (f32[256,768]{1,0:T(8,128)}, f32[256,768]{1,0:T(8,128)}) async-done(((f32[256,768]{1,0:T(8,128)}, f32[256,768]{1,0:T(8,128)}), (f32[256,768]{1,0:T(8,128)}, f32[256,768]{1,0:T(8,128)})) %all-reduce.13.cloned.1.call-update) | async-done | bytes 1572880 | tf_op jit(solution)/shard_map/psum | solution.py:166
  381.0 3.2 multiply_reduce_fusion.3
  392.3 8.2 %fusion.12 = f32[3,64,1024]{2,1,0:T(8,128)} fusion(f32[3,256,1024]{2,1,0:T(8,128)} %fusion.208, f32[3,256,1024]{2,1,0:T(8,128)S(1)} %get-tuple-element.197, f32[3,256]{1,0:T(4,128)} %log_add_fusion.1, f32[256,3,64]{0,2,1:T(8,128)} %bitcast.265, f32[3,64]{1,0:T(4,128)} %copy-done.71), kind=kOutput, calls=%fused_computation.19 | convolution fusion | flops 106268416 | bytes 7278336 | tf_op jit(solution)/shard_map/hqk,qhd->khd/dot_general | solution.py:190
  407.0 3.3 fusion.209
  410.3 9.9 %fusion.19 = f32[3,64,1024]{2,1,0:T(8,128)} fusion(f32[3,256,1024]{2,1,0:T(8,128)} %fusion.209, f32[3,256,1024]{2,1,0:T(8,128)} %copy-done, f32[3,256]{1,0:T(4,128)S(1)} %copy-done.81, f32[256,3,64]{0,2,1:T(8,128)S(1)} %bitcast.263, f32[3,64]{1,0:T(4,128)S(1)} %copy-done.73), kind=kOutput, calls=%fused_computation.22 | convolution fusion | flops 106268416 | bytes 7278336 | tf_op jit(solution)/shard_map/hqk,qhd->khd/dot_general | solution.py:190
  428.9 9.9 %fusion.194 = (f32[3,64]{1,0:T(4,128)}, bf16[256,3,64]{0,2,1:T(8,128)(2,1)}) fusion(bf16[1024,3,64]{0,2,1:T(8,128)(2,1)} %bitcast.248, f32[3,256,1024]{2,1,0:T(8,128)} %fusion.209, f32[3,256,1024]{2,1,0:T(8,128)} %copy-done, f32[3,256]{1,0:T(4,128)} %log_add_fusion), kind=kOutput, calls=%fused_computation.286 | convolution fusion | flops 106268224 | bytes 6786816 | tf_op jit(solution)/shard_map/hqk,khd->qhd/dot_general | solution.py:187
  438.8 8.0 %fusion.195 = (f32[3,64]{1,0:T(4,128)}, bf16[256,3,64]{0,2,1:T(8,128)(2,1)}) fusion(bf16[1024,3,64]{0,2,1:T(8,128)(2,1)S(1)} %bitcast.247, f32[3,256,1024]{2,1,0:T(8,128)} %fusion.208, f32[3,256,1024]{2,1,0:T(8,128)S(1)} %get-tuple-element.197, f32[3,256]{1,0:T(4,128)S(1)} %copy-done.80), kind=kOutput, calls=%fused_computation.287 | convolution fusion | flops 106268224 | bytes 6786816 | tf_op jit(solution)/shard_map/hqk,khd->qhd/dot_general | solution.py:187
  451.2 24.1 %reduce-scatter.16.cloned.1.call-done = f32[256,384]{0,1:T(8,128)} async-done(((f32[1024,384]{0,1:T(8,128)}), f32[256,384]{0,1:T(8,128)}) %reduce-scatter.16.cloned.1.call-update) | async-done | bytes 393232 | tf_op jit(solution)/shard_map/reduce_scatter | solution.py:196
  509.7 38.1 %all-reduce.11.cloned.1.call-done = (f32[256,768]{1,0:T(8,128)}, f32[256,768]{1,0:T(8,128)}, f32[256,768]{1,0:T(8,128)}, f32[256,768]{1,0:T(8,128)}) async-done(((f32[256,768]{1,0:T(8,128)}, f32[256,768]{1,0:T(8,128)}, f32[256,768]{1,0:T(8,128)}, f32[256,768]{1,0:T(8,128)}), (f32[256,768]{1,0:T(8,128)}, f32[256,768]{1,0:T(8,128)}, f32[256,768]{1,0:T(8,128)}, ...) | async-done | bytes 3145744 | tf_op jit(solution)/shard_map/psum | solution.py:118
  550.4 29.9 %all-reduce.9.cloned.1.call-done = (f32[9216]{0:T(1024)}, f32[9216]{0:T(1024)}) async-done(((f32[9216]{0:T(1024)}, f32[9216]{0:T(1024)}), (f32[9216]{0:T(1024)}, f32[9216]{0:T(1024)})) %all-reduce.9.cloned.1.call-update) | async-done | bytes 73744 | tf_op jit(solution)/shard_map/psum | solution.py:233
  582.2 3.3 add_bitcast_fusion
  585.5 4.2 copy.84
  589.7 4.8 reshape.400
  601.7 26.3 %reduce-scatter.18.cloned.1.call-done = f32[96,768]{1,0:T(8,128)} async-done(((f32[768,768]{1,0:T(8,128)}), f32[96,768]{1,0:T(8,128)}) %reduce-scatter.18.cloned.1.call-update) | async-done | bytes 294928 | tf_op jit(solution)/shard_map/reduce_scatter | solution.py:285
  637.6 54.3 %reduce-scatter.26.cloned.1.call-done = f32[96,12]{1,0:T(8,128)} async-done(((f32[768,12]{1,0:T(8,128)}), f32[96,12]{1,0:T(8,128)}) %reduce-scatter.26.cloned.1.call-update) | async-done | bytes 4624
  693.4 68.1 %reduce-scatter.22.cloned.1.call-done = f32[96,576]{1,0:T(8,128)} async-done(((f32[768,576]{1,0:T(8,128)}), f32[96,576]{1,0:T(8,128)}) %reduce-scatter.22.cloned.1.call-update) | async-done | bytes 221200
  (373 shorter events, 137.0 us)
Async XLA Ops:
  8.0 76.9 %copy-start.1 = (bf16[2,256,768]{2,1,0:T(8,128)(2,1)S(1)}, bf16[2,256,768]{2,1,0:T(8,128)(2,1)}, u32[]{:S(2)}) copy-start(bf16[2,256,768]{2,1,0:T(8,128)(2,1)} %param.18) | copy-start | bytes 2359300
  8.0 199.6 %all-reduce.15.cloned.1.call-start = ((), (), s32[]{:S(2)}) async-start(), calls=%async_computation.19 | async-start | bytes 3145728 | tf_op jit(solution)/shard_map/psum | solution.py:110
  43.0 43.6 %copy-start.58 = (f32[768]{0:T(1024)}, f32[768]{0:T(1024)S(1)}, u32[]{:S(2)}) copy-start(f32[768]{0:T(1024)S(1)} %get-tuple-element.176) | copy-start | bytes 9220
  105.5 51.3 %copy-start.71 = (f32[3,64]{1,0:T(4,128)}, f32[3,64]{1,0:T(4,128)S(1)}, u32[]{:S(2)}) copy-start(f32[3,64]{1,0:T(4,128)S(1)} %add.429) | copy-start | bytes 2308
  164.3 47.5 %all-gather.4.cloned.1.call-start = ((), (), s32[]{:S(2)}) async-start(), calls=%async_computation.7 | async-start | bytes 1327104 | tf_op jit(solution)/shard_map/all_gather | solution.py:41
  166.0 122.7 %reduce-scatter.20.cloned.1.call-start = ((), (), s32[]{:S(2)}) async-start(), calls=%async_computation.12 | async-start | bytes 2654208 | tf_op jit(solution)/shard_map/reduce_scatter | solution.py:286
  219.4 112.5 %all-gather.6.cloned.1.call-start = ((), (), s32[]{:S(2)}) async-start(), calls=%async_computation.8 | async-start | bytes 1327104 | tf_op jit(solution)/shard_map/all_gather | solution.py:42
  291.2 89.8 %all-reduce.13.cloned.1.call-start = ((), (), s32[]{:S(2)}) async-start(), calls=%async_computation.18 | async-start | bytes 3145728 | tf_op jit(solution)/shard_map/psum | solution.py:166
  339.3 107.6 %reduce-scatter.14.cloned.1.call-start = ((), (), s32[]{:S(2)}) async-start(), calls=%async_computation.9 | async-start | bytes 1966080 | tf_op jit(solution)/shard_map/reduce_scatter | solution.py:196
  403.3 72.0 %reduce-scatter.16.cloned.1.call-start = ((), (), s32[]{:S(2)}) async-start(), calls=%async_computation.10 | async-start | bytes 1966080 | tf_op jit(solution)/shard_map/reduce_scatter | solution.py:196
  424.2 123.6 %all-reduce.11.cloned.1.call-start = ((), (), s32[]{:S(2)}) async-start(), calls=%async_computation.17 | async-start | bytes 6291456 | tf_op jit(solution)/shard_map/psum | solution.py:118
  479.6 100.7 %all-reduce.9.cloned.1.call-start = ((), (), s32[]{:S(2)}) async-start(), calls=%async_computation.16 | async-start | bytes 147456 | tf_op jit(solution)/shard_map/psum | solution.py:233
  490.4 107.9 %reduce-scatter.24.cloned.1.call-start = ((), (), s32[]{:S(2)}) async-start(), calls=%async_computation.14 | async-start | bytes 884736
  493.8 134.1 %reduce-scatter.18.cloned.1.call-start = ((), (), s32[]{:S(2)}) async-start(), calls=%async_computation.11 | async-start | bytes 2654208 | tf_op jit(solution)/shard_map/reduce_scatter | solution.py:285
  498.8 83.4 %copy-start.52 = (bf16[1,256,192]{1,2,0:T(8,128)(2,1)S(1)}, bf16[1,256,192]{1,2,0:T(8,128)(2,1)}, u32[]{:S(2)}) copy-start(bf16[1,256,192]{1,2,0:T(8,128)(2,1)} %copy-done.51) | copy-start | bytes 294916
  498.8 83.4 %copy-start.54 = (bf16[1,256,192]{1,2,0:T(8,128)(2,1)S(1)}, bf16[1,256,192]{1,2,0:T(8,128)(2,1)}, u32[]{:S(2)}) copy-start(bf16[1,256,192]{1,2,0:T(8,128)(2,1)} %copy-done.53) | copy-start | bytes 294916
  498.8 193.1 %reduce-scatter.26.cloned.1.call-start = ((), (), s32[]{:S(2)}) async-start(), calls=%async_computation.15 | async-start | bytes 442368
  509.6 72.5 %copy-start.57 = (bf16[256,3,64]{0,2,1:T(8,128)(2,1)S(1)}, bf16[256,3,64]{0,2,1:T(8,128)(2,1)}, u32[]{:S(2)}) copy-start(bf16[256,3,64]{0,2,1:T(8,128)(2,1)} %get-tuple-element.170) | copy-start | bytes 294916
  582.1 179.4 %reduce-scatter.22.cloned.1.call-start = ((), (), s32[]{:S(2)}) async-start(), calls=%async_computation.13 | async-start | bytes 2211840
  631.7 61.1 %copy-start.60 = (f32[12,96]{1,0:T(8,128)S(1)}, f32[12,96]{1,0:T(8,128)}, u32[]{:S(2)}) copy-start(f32[12,96]{1,0:T(8,128)} %param.33) | copy-start | bytes 13828
  631.7 61.1 %copy-start.93 = (f32[12,96]{1,0:T(8,128)S(1)}, f32[12,96]{1,0:T(8,128)}, u32[]{:S(2)}) copy-start(f32[12,96]{1,0:T(8,128)} %param.34) | copy-start | bytes 13828
  631.7 61.1 %copy-start.94 = (f32[12,96]{1,0:T(8,128)S(1)}, f32[12,96]{1,0:T(8,128)}, u32[]{:S(2)}) copy-start(f32[12,96]{1,0:T(8,128)} %param.35) | copy-start | bytes 13828
  633.7 129.1 %copy-start.29 = (f32[3,96,192]{1,2,0:T(8,128)S(1)}, f32[3,96,192]{1,2,0:T(8,128)}, u32[]{:S(2)}) copy-start(f32[3,96,192]{1,2,0:T(8,128)} %copy.80) | copy-start | bytes 663556
  633.7 129.1 %copy-start.30 = (f32[3,96,192]{1,2,0:T(8,128)S(1)}, f32[3,96,192]{1,2,0:T(8,128)}, u32[]{:S(2)}) copy-start(f32[3,96,192]{1,2,0:T(8,128)} %copy.78) | copy-start | bytes 663556
  (90 other events, 597.5 us)
Sparse Core Ops, SparseCore 0:
  164.4 43.1 all-reduce.14
  339.4 41.5 all-reduce.12
  403.4 35.3 reduce-scatter.13
  441.0 34.2 reduce-scatter.15
  479.8 67.9 all-reduce.10
  550.7 29.5 all-reduce.8
Sparse Core Ops, SparseCore 1:
  167.5 41.4 all-gather.3
  219.4 69.2 reduce-scatter.19
  291.3 40.6 all-gather.5
  494.5 61.7 reduce-scatter.23
  560.1 67.8 reduce-scatter.17
  631.3 60.6 reduce-scatter.25
  695.2 66.3 reduce-scatter.21
where the time goes:
time: 782 us; the launch traced here: 774 us
  waiting for transfers between devices  429 us (55%)
  blocking collectives  136 us (17%)
  matrix products  90.3 us (12%)
  local copies, waits for them, and re-layouts  55.8 us (7%)
  other arithmetic  44.4 us (6%)
  between operations  17.3 us (2%)
    unnamed x16, waiting for transfers between devices  123 us
    reduce_scatter x1, waiting for transfers between devices, on_device(): lax.psum_scatter(totals[3], ('dp', 'ctx'), scatter_dimension=1, tiled=True)  69.3 us
    all_gather x1, waiting for transfers between devices, fetch_rows(): lax.all_gather(masters[3].astype(jnp.bfloat16), ('dp', 'ctx'), axis=1, ti...  40.7 us
    psum x1, waiting for transfers between devices, backward_pass(): second_grad = lax.psum(second_part, 'tensor')  40.3 us
    all_gather x1, blocking collectives, fetch_rows(): lax.all_gather(masters[0].astype(jnp.bfloat16), ('dp', 'ctx'), axis=1, ti...  39.8 us
    psum x1, waiting for transfers between devices, forward_pass(): result = share_rows(middle + lax.psum(down_part, 'tensor') + table[7])  38.1 us
    psum x1, waiting for transfers between devices, forward_pass(): middle = inputs + lax.psum(attn_part, 'tensor') + table[4]  37.4 us
    all_gather x1, blocking collectives, fetch_rows(): lax.all_gather(masters[4].astype(jnp.bfloat16), ('dp', 'ctx'), axis=1, ti...  32.1 us
  transfers between devices with their start and end apart: 13, of which 10 were waited for; matrix products, arithmetic and copies ran while one was open for 16% of the time, Pallas kernels for 0%

commit v1 on v0

v1 whole, which is shorter than its diff:
```python
import jax
import jax.numpy as jnp
from jax import lax
from jax.sharding import PartitionSpec as P

HD = 64
STEP = 10

norm_eps = 1e-05
beta_first = 0.9
beta_second = 0.999
adam_eps = 1e-08
weight_decay = 0.01
rate_qkv = 0.05
rate_out = 0.2
rate_up = 0.05
rate_down = 0.025
rate_vectors = 0.3

LOW = jnp.bfloat16
F32 = jnp.float32


def dot(left, right, left_dim, right_dim):
    return lax.dot_general(
        left, right, (((left_dim,), (right_dim,)), ((), ())), preferred_element_type=F32
    )


def unit_norm(values):
    centre = values - jnp.mean(values, axis=-1, keepdims=True)
    scale = lax.rsqrt(jnp.mean(centre * centre, axis=-1, keepdims=True) + norm_eps)
    return centre * scale, scale


def norm_back(grad, gain, unit, scale):
    inner = grad * gain
    return scale * (
        inner
        - jnp.mean(inner, axis=-1, keepdims=True)
        - unit * jnp.mean(inner * unit, axis=-1, keepdims=True)
    )


def adamw(weight, first, second, grad, rate, decay):
    first_new = beta_first * first + (1.0 - beta_first) * grad
    second_new = beta_second * second + (1.0 - beta_second) * grad * grad
    fix_first = 1.0 - beta_first**STEP
    fix_second = 1.0 - beta_second**STEP
    update = first_new / fix_first / (jnp.sqrt(second_new / fix_second) + adam_eps)
    return (weight - rate * (update + decay * weight), first_new, second_new)


def gather_weights(shard):
    return lax.all_gather(shard, ("dp", "ctx"), axis=0, tiled=True)


def scatter_grads(grads):
    return lax.psum_scatter(grads, ("dp", "ctx"), scatter_dimension=0, tiled=True)


def gather_ctx(values):
    return lax.all_gather(values, "ctx", axis=1, tiled=True)


def scatter_ctx(values):
    return lax.psum_scatter(values, "ctx", scatter_dimension=1, tiled=True)


def gather_tensor(values):
    return lax.all_gather(values, "tensor", axis=1, tiled=True)


def scatter_tensor(values):
    return lax.psum_scatter(values, "tensor", scatter_dimension=1, tiled=True)


def my_rows(values):
    part = values.shape[1] // lax.axis_size("tensor")
    return lax.dynamic_slice_in_dim(values, lax.axis_index("tensor") * part, part, 1)


def allowed_pairs(segment, tokens):
    ctx_index = lax.axis_index("ctx")
    key_places = jnp.arange(segment.shape[1], dtype=jnp.int32)
    query_places = ctx_index * tokens + jnp.arange(tokens, dtype=jnp.int32)
    query_segment = lax.dynamic_slice_in_dim(segment, ctx_index * tokens, tokens, 1)
    return (query_places[None, :, None] >= key_places[None, None, :]) & (
        query_segment[:, :, None] == segment[:, None, :]
    )


def heads_of(values):
    batch, tokens, width = values.shape
    return values.reshape(batch, tokens, width // HD, HD)


def attend(query, keys, values, allowed):
    scores = jnp.einsum(
        "bqhd,bkhd->bhqk", heads_of(query), heads_of(keys), preferred_element_type=F32
    ) * HD ** (-0.5)
    scores = jnp.where(allowed[:, None], scores, -1e30)
    weights = jnp.exp(scores - jnp.max(scores, axis=-1, keepdims=True))
    probs = weights / jnp.sum(weights, axis=-1, keepdims=True)
    mixed = jnp.einsum(
        "bhqk,bkhd->bqhd", probs.astype(LOW), heads_of(values), preferred_element_type=F32
    )
    return mixed.reshape(query.shape).astype(LOW), probs


def attend_back(mixed_grad, query, keys, values, probs):
    grad_heads = heads_of(mixed_grad)
    prob_grad = jnp.einsum(
        "bqhd,bkhd->bhqk", grad_heads, heads_of(values), preferred_element_type=F32
    )
    row_delta = jnp.sum(prob_grad * probs, axis=-1, keepdims=True)
    score_grad = (probs * (prob_grad - row_delta) * HD ** (-0.5)).astype(LOW)
    query_grad = jnp.einsum(
        "bhqk,bkhd->bqhd", score_grad, heads_of(keys), preferred_element_type=F32
    ).reshape(query.shape)
    key_grad = jnp.einsum(
        "bhqk,bqhd->bkhd", score_grad, heads_of(query), preferred_element_type=F32
    ).reshape(keys.shape)
    value_grad = jnp.einsum(
        "bhqk,bqhd->bkhd", probs.astype(LOW), grad_heads, preferred_element_type=F32
    ).reshape(keys.shape)
    return query_grad, key_grad, value_grad


def on_device(
    hidden_in,
    cotangent,
    segment_ids,
    qkv_weight,
    qkv_first,
    qkv_second,
    out_weight,
    out_first,
    out_second,
    up_weight,
    up_first,
    up_second,
    down_weight,
    down_first,
    down_second,
    vectors,
    vectors_first,
    vectors_second,
):
    batch, tokens, model = hidden_in.shape
    width = qkv_weight.shape[2]
    units = up_weight.shape[1]
    rows_all = batch * tokens
    tensor_index = lax.axis_index("tensor")

    attn_shard = jnp.concatenate(
        [qkv_weight[0], qkv_weight[1], qkv_weight[2]], axis=1
    ).astype(LOW)
    rest_shard = jnp.concatenate([out_weight.T, up_weight, down_weight.T], axis=1).astype(LOW)
    table = lax.all_gather(
        vectors.astype(LOW), ("dp", "ctx"), axis=1, tiled=True
    ).astype(F32)
    proj = gather_weights(attn_shard)
    rest = gather_weights(rest_shard)
    out_turned = rest[:, :width]
    up = rest[:, width : width + units]
    down_turned = rest[:, width + units :]

    inputs = hidden_in.astype(F32)
    unit_first, scale_first = unit_norm(inputs)
    first_norm = (unit_first * table[0] + table[1]).astype(LOW).reshape(rows_all, model)
    projected = dot(first_norm, proj, 1, 0)
    query_bias = lax.dynamic_slice_in_dim(table[2], tensor_index * width, width)
    value_bias = lax.dynamic_slice_in_dim(table[3], tensor_index * width, width)
    query = (projected[:, :width] + query_bias).astype(LOW).reshape(batch, tokens, width)
    local_kv = (
        jnp.concatenate([projected[:, width : 2 * width], projected[:, 2 * width :] + value_bias], axis=1)
        .astype(LOW)
        .reshape(batch, tokens, 2 * width)
    )
    all_kv = gather_ctx(local_kv)
    keys, values = all_kv[..., :width], all_kv[..., width:]
    allowed = allowed_pairs(segment_ids, tokens)
    mixed, probs = attend(query, keys, values, allowed)
    mixed = mixed.reshape(rows_all, width)

    attn_part = dot(mixed, out_turned, 1, 1).astype(LOW).reshape(batch, tokens, model)
    middle = my_rows(inputs) + scatter_tensor(attn_part).astype(F32) + table[4]
    unit_second, scale_second = unit_norm(middle)
    second_norm = gather_tensor((unit_second * table[5] + table[6]).astype(LOW))
    second_norm = second_norm.reshape(rows_all, model)
    unit_bias = lax.dynamic_slice_in_dim(table[8:].reshape(-1), tensor_index * units, units)
    hidden = dot(second_norm, up, 1, 0) + unit_bias
    gelu_value, gelu_pull = jax.vjp(jax.nn.gelu, hidden)
    active = gelu_value.astype(LOW)
    down_part = dot(active, down_turned, 1, 1).astype(LOW).reshape(batch, tokens, model)
    result = (middle + scatter_tensor(down_part).astype(F32) + table[7]).astype(LOW)

    back = cotangent.reshape(rows_all, model)
    back_rows = my_rows(cotangent).astype(F32)
    hidden_grad = gelu_pull(dot(back, down_turned, 1, 0))[0]
    hidden_low = hidden_grad.astype(LOW)
    second_part = dot(hidden_low, up, 1, 1).astype(LOW).reshape(batch, tokens, model)
    second_grad = scatter_tensor(second_part).astype(F32)
    grad_down = dot(back, active, 0, 0)
    grad_up = dot(second_norm, hidden_low, 0, 0)
    late_sum = scatter_grads(jnp.concatenate([grad_up, grad_down], axis=1).astype(LOW))

    middle_grad = back_rows + norm_back(second_grad, table[5], unit_second, scale_second)
    middle_low = gather_tensor(middle_grad.astype(LOW)).reshape(rows_all, model)
    mixed_grad = dot(middle_low, out_turned, 1, 0).astype(LOW).reshape(batch, tokens, width)
    query_grad, key_part, value_part = attend_back(mixed_grad, query, keys, values, probs)
    kv_grad = scatter_ctx(jnp.concatenate([key_part, value_part], axis=2).astype(LOW))
    grad_out = dot(middle_low, mixed, 0, 0)
    stacked = jnp.concatenate([query_grad.astype(LOW), kv_grad], axis=2).reshape(
        rows_all, 3 * width
    )
    first_part = dot(stacked, proj, 1, 1).astype(LOW).reshape(batch, tokens, model)
    first_grad = scatter_tensor(first_part).astype(F32)
    grad_qkv = dot(first_norm, stacked, 0, 0)
    early_sum = scatter_grads(jnp.concatenate([grad_qkv, grad_out], axis=1).astype(LOW))
    my_unit, my_scale = my_rows(unit_first), my_rows(scale_first)
    input_grad = middle_grad + norm_back(first_grad, table[0], my_unit, my_scale)

    def total(values):
        return jnp.sum(values, axis=(0, 1))

    owned = jnp.zeros((vectors.shape[0] * model,), F32)
    owned = lax.dynamic_update_slice(
        owned, total(query_grad), (2 * model + tensor_index * width,)
    )
    owned = lax.dynamic_update_slice(
        owned, total(value_part), (3 * model + tensor_index * width,)
    )
    owned = lax.dynamic_update_slice(
        owned, jnp.sum(hidden_grad, axis=0), (8 * model + tensor_index * units,)
    )
    zero = jnp.zeros((model,), F32)
    rows = jnp.stack(
        [total(first_grad * my_unit), total(first_grad), zero, zero]
        + [total(middle_grad), total(second_grad * unit_second)]
        + [total(second_grad), total(back_rows)]
        + [zero] * (vectors.shape[0] - 8)
    )
    grad_table = lax.psum(owned.reshape(rows.shape) + rows, ("dp", "ctx", "tensor"))
    part = vectors.shape[1]
    grad_vectors = lax.dynamic_slice_in_dim(
        grad_table,
        (lax.axis_index("dp") * lax.axis_size("ctx") + lax.axis_index("ctx")) * part,
        part,
        1,
    )

    early_sum = early_sum.astype(F32)
    late_sum = late_sum.astype(F32)
    qkv_sum = jnp.stack([early_sum[:, place * width : (place + 1) * width] for place in range(3)])
    out_sum = early_sum[:, 3 * width :].T
    up_sum = late_sum[:, :units]
    down_sum = late_sum[:, units:].T
    return (
        result,
        input_grad,
        *adamw(qkv_weight, qkv_first, qkv_second, qkv_sum, rate_qkv, weight_decay),
        *adamw(out_weight, out_first, out_second, out_sum, rate_out, weight_decay),
        *adamw(up_weight, up_first, up_second, up_sum, rate_up, weight_decay),
        *adamw(down_weight, down_first, down_second, down_sum, rate_down, weight_decay),
        *adamw(vectors, vectors_first, vectors_second, grad_vectors, rate_vectors, 0.0),
    )


def solution(mesh):
    tokens = P("dp", "ctx", None)
    shares = P("dp", ("ctx", "tensor"), None)
    by_row = P(("dp", "ctx"), "tensor")
    by_column = P("tensor", ("dp", "ctx"))
    stacked = P(None, ("dp", "ctx"), "tensor")
    narrow = P(None, ("dp", "ctx"))
    states = (stacked,) * 3 + (by_column,) * 3 + (by_row,) * 3 + (by_column,) * 3 + (narrow,) * 3
    return jax.shard_map(
        on_device,
        mesh=mesh,
        in_specs=(tokens, tokens, P("dp", None)) + states,
        out_specs=(shares, shares) + states,
        check_vma=False,
    )
```

time: 782 us -> 519 us (0.66)
  waiting for transfers between devices: 429 us -> 262 us
  local copies, waits for them, and re-layouts: 55.8 us -> 22.5 us
  matrix products: 90.3 us -> 69.9 us
  other arithmetic: 44.4 us -> 25.3 us
  blocking collectives: 136 us -> 123 us
    psum x4 -> x0, waiting for transfers between devices: 146 us -> none  [the longest x1 40.3 us: backward_pass(): second_grad = lax.psum(second_part, 'tensor')]
    unnamed x16 -> x10, waiting for transfers between devices: 123 us -> 23.7 us
    all_gather x5 -> x4, blocking collectives: 136 us -> 82.9 us  [the longest x1 34.2 us: gather_weights(): return lax.all_gather(shard, ('dp', 'ctx'), axis=0, tiled=True)]
    psum x0 -> x1, blocking collectives: none -> 40.2 us  [on_device(): lax.psum(owned.reshape(rows.shape) + rows, ('dp', 'ctx', 'tensor'))]
    all_gather x2, waiting for transfers between devices: 40.7 us -> 80.6 us  [the longest x1 43.4 us: gather_weights(): return lax.all_gather(shard, ('dp', 'ctx'), axis=0, tiled=True)]
    reduce_scatter x4 -> x6, waiting for transfers between devices: 120 us -> 158 us  [the longest x4 85.1 us: scatter_tensor(): return lax.psum_scatter(values, 'tensor', scatter_dimension=1, tiled=True)]
    dot_general x34 -> x17, matrix products: 89.2 us -> 64.8 us  [the longest x12 18.9 us: dot(): lax.dot_general(left, right, (((left_dim,), (right_dim,)), ((), ())), pre...]
    unnamed x217 -> x117, local copies, waits for them, and re-layouts: 29.2 us -> 14.3 us
  transfers between devices with their start and end apart: 13 -> 9, of which waited for: 10 -> 9; matrix products, arithmetic and copies ran while one was open for 16% -> 12% of each run, Pallas kernels for 0% -> 0%
where the time goes in v1:
time: 519 us; the launch traced here: 518 us
  waiting for transfers between devices  262 us (50%)
  blocking collectives  123 us (24%)
  matrix products  69.9 us (13%)
  other arithmetic  25.3 us (5%)
  local copies, waits for them, and re-layouts  22.5 us (4%)
  between operations  14.7 us (3%)
    reduce_scatter x4, waiting for transfers between devices, scatter_tensor(): return lax.psum_scatter(values, 'tensor', scatter_dimension=1, tiled=True)  85.1 us
    reduce_scatter x1, waiting for transfers between devices, scatter_grads(): lax.psum_scatter(grads, ('dp', 'ctx'), scatter_dimension=0, tiled=True)  60.6 us
    all_gather x1, waiting for transfers between devices, gather_weights(): return lax.all_gather(shard, ('dp', 'ctx'), axis=0, tiled=True)  43.4 us
    psum x1, blocking collectives, on_device(): lax.psum(owned.reshape(rows.shape) + rows, ('dp', 'ctx', 'tensor'))  40.2 us
    all_gather x1, waiting for transfers between devices, gather_ctx(): return lax.all_gather(values, 'ctx', axis=1, tiled=True)  37.1 us
    all_gather x1, blocking collectives, gather_weights(): return lax.all_gather(shard, ('dp', 'ctx'), axis=0, tiled=True)  34.2 us
    all_gather x1, blocking collectives, on_device(): lax.all_gather(vectors.astype(LOW), ('dp', 'ctx'), axis=1, tiled=True)  32.1 us
    unnamed x10, waiting for transfers between devices  23.7 us
  transfers between devices with their start and end apart: 9, of which 9 were waited for; matrix products, arithmetic and copies ran while one was open for 12% of the time, Pallas kernels for 0%

profile of v1, /device:TPU:0, one launch (start us, length us, event | category | flops | bytes accessed | tf_op | source)
XLA Modules:
  0.0 518.1 jit_solution(11544694243449524134)
XLA Ops:
  10.3 32.1 %all-gather = bf16[8,96,12]{1,2,0:T(8,128)(2,1)S(1)} all-gather(bf16[1,96,12]{1,2,0:T(8,128)(2,1)S(1)} %convert_bitcast_fusion.2), channel_id=1, replica_groups=mesh['dp'=2,'ctx'=4,'tensor'=4] {'dp','ctx'}, dimensions={0}, use_global_device_ids=true | all-gather | bytes 20736 | tf_op jit(solution)/shard_map/all_gather | solution.py:160
  43.3 34.2 %all_gather.19 = bf16[768,576]{1,0:T(8,128)(2,1)S(1)} all-gather(bf16[96,576]{1,0:T(8,128)(2,1)S(1)} %pad_maximum_fusion.7), channel_id=1, replica_groups=mesh['dp'=2,'ctx'=4,'tensor'=4] {'dp','ctx'}, dimensions={0}, use_global_device_ids=true | all-gather | bytes 995328 | tf_op jit(solution)/shard_map/all_gather | solution.py:55
  83.6 37.1 %all-gather.4.cloned.1.call-done = bf16[2,1024,384]{1,0,2:T(2,128)(2,1)} async-done(((bf16[2,256,384]{1,0,2:T(2,128)(2,1)}), bf16[2,1024,384]{1,0,2:T(2,128)(2,1)}) %all-gather.4.cloned.1.call-update) | async-done | bytes 1572880 | tf_op jit(solution)/shard_map/all_gather | solution.py:63
  120.7 2.4 fusion.99
  123.6 5.1 fusion.102
  128.7 4.1 fusion.38
  133.7 43.4 %all-gather.6.cloned.1.call-done = bf16[768,1728]{1,0:T(8,128)(2,1)} async-done(((bf16[96,1728]{1,0:T(8,128)(2,1)}), bf16[768,1728]{1,0:T(8,128)(2,1)}) %all-gather.6.cloned.1.call-update) | async-done | bytes 2654224 | tf_op jit(solution)/shard_map/all_gather | solution.py:55
  179.8 21.8 %reduce-scatter.12.cloned.1.call-done = bf16[2,64,768]{2,1,0:T(8,128)(2,1)} async-done(((bf16[2,256,768]{2,1,0:T(8,128)(2,1)}), bf16[2,64,768]{2,1,0:T(8,128)(2,1)}) %reduce-scatter.12.cloned.1.call-update) | async-done | bytes 196624 | tf_op jit(solution)/shard_map/reduce_scatter | solution.py:75
  203.2 8.4 %all_gather.22 = bf16[2,256,768]{2,1,0:T(8,128)(2,1)S(1)} all-gather(bf16[2,64,768]{2,1,0:T(8,128)(2,1)S(1)} %add_convert_fusion.2), channel_id=1, replica_groups=mesh['dp'=2,'ctx'=4,'tensor'=4] {'tensor'}, dimensions={1}, use_global_device_ids=true | all-gather | bytes 983040 | tf_op jit(solution)/shard_map/all_gather | solution.py:71
  217.0 4.0 convolution_convert_fusion.3
  221.0 19.7 %reduce-scatter.16.cloned.1.call-done = bf16[2,64,768]{2,1,0:T(8,128)(2,1)} async-done(((bf16[2,256,768]{2,1,0:T(8,128)(2,1)}), bf16[2,64,768]{2,1,0:T(8,128)(2,1)}) %reduce-scatter.16.cloned.1.call-update) | async-done | bytes 196624 | tf_op jit(solution)/shard_map/reduce_scatter | solution.py:75
  242.5 23.9 %reduce-scatter.14.cloned.1.call-done = bf16[2,64,768]{2,1,0:T(8,128)(2,1)} async-done(((bf16[2,256,768]{2,1,0:T(8,128)(2,1)}), bf16[2,64,768]{2,1,0:T(8,128)(2,1)}) %reduce-scatter.14.cloned.1.call-update) | async-done | bytes 196624 | tf_op jit(solution)/shard_map/reduce_scatter | solution.py:75
  266.4 2.5 fusion.93
  269.0 8.2 %all_gather.23 = bf16[2,256,768]{2,1,0:T(8,128)(2,1)S(1)} all-gather(bf16[2,64,768]{2,1,0:T(8,128)(2,1)S(1)} %convert_element_type.120), channel_id=1, replica_groups=mesh['dp'=2,'ctx'=4,'tensor'=4] {'tensor'}, dimensions={1}, use_global_device_ids=true | all-gather | bytes 983040 | tf_op jit(solution)/shard_map/all_gather | solution.py:71
  279.3 4.8 bitcast_convert_fusion.1
  284.1 3.7 fusion.73
  287.7 17.1 %fusion.31 = bf16[2,3,64,1024]{3,2,1,0:T(8,128)(2,1)S(1)} fusion(f32[2,3,256,1024]{3,2,1,0:T(8,128)} %fusion.73, bf16[2,256,3,64]{1,0,3,2:T(2,128)(2,1)} %copy-done.27, f32[2,3,256,1024]{3,2,1,0:T(8,128)} %get-tuple-element.143, f32[2,3,256]{2,1,0:T(4,128)} %copy-done.51), kind=kOutput, calls=%fused_computation.51 | convolution fusion | flops 212732416 | bytes 13572096 | tf_op jit(solution)/shard_map/bhqk,bqhd->bkhd/dot_general | solution.py:121
  309.8 2.5 copy.145
  313.5 16.4 %fusion.100 = (f32[3,64]{1,0:T(4,128)}, bf16[2,256,3,64]{1,3,2,0:T(8,128)(2,1)S(1)}) fusion(bf16[2,1024,3,64]{1,3,2,0:T(8,128)(2,1)S(1)} %bitcast.132, f32[2,3,256,1024]{3,2,1,0:T(8,128)} %fusion.73, f32[2,3,256,1024]{3,2,1,0:T(8,128)} %get-tuple-element.143, f32[2,3,256]{2,1,0:T(4,128)S(1)} %copy-done.52), kind=kOutput, calls=%fused_computation.175 | convolution fusion | flops 212535616 | bytes 13572864 | tf_op jit(solution)/shard_map/bhqk,bkhd->bqhd/dot_general | solution.py:118
  329.8 12.1 %reduce-scatter.18.cloned.1.call-done = bf16[2,256,384]{1,2,0:T(8,128)(2,1)} async-done(((bf16[2,1024,384]{1,2,0:T(8,128)(2,1)}), bf16[2,256,384]{1,2,0:T(8,128)(2,1)}) %reduce-scatter.18.cloned.1.call-update) | async-done | bytes 393232 | tf_op jit(solution)/shard_map/reduce_scatter | solution.py:67
  353.6 60.6 %reduce-scatter.24.cloned.1.call-done = bf16[96,1536]{1,0:T(8,128)(2,1)} async-done(((bf16[768,1536]{1,0:T(8,128)(2,1)}), bf16[96,1536]{1,0:T(8,128)(2,1)}) %reduce-scatter.24.cloned.1.call-update) | async-done | bytes 294928 | tf_op jit(solution)/shard_map/reduce_scatter | solution.py:59
  419.5 19.6 %reduce-scatter.20.cloned.1.call-done = bf16[2,64,768]{2,1,0:T(8,128)(2,1)} async-done(((bf16[2,256,768]{2,1,0:T(8,128)(2,1)}), bf16[2,64,768]{2,1,0:T(8,128)(2,1)}) %reduce-scatter.20.cloned.1.call-update) | async-done | bytes 196624 | tf_op jit(solution)/shard_map/reduce_scatter | solution.py:75
  440.4 40.2 %psum.7 = f32[12,768]{1,0:T(8,128)S(1)} all-reduce(f32[12,768]{1,0:T(8,128)S(1)} %add.314), channel_id=1, replica_groups=mesh['dp'=2,'ctx'=4,'tensor'=4] {'dp','ctx','tensor'}, use_global_device_ids=true, to_apply=%region_27.28 | all-reduce | flops 9216 | bytes 73728 | tf_op jit(solution)/shard_map/psum | solution.py:245
  483.3 23.5 %reduce-scatter.22.cloned.1.call-done = bf16[96,768]{1,0:T(8,128)(2,1)} async-done(((bf16[768,768]{1,0:T(8,128)(2,1)}), bf16[96,768]{1,0:T(8,128)(2,1)}) %reduce-scatter.22.cloned.1.call-update) | async-done | bytes 147472
  (224 shorter events, 56.0 us)
Async XLA Ops:
  7.2 35.9 %copy-start.7 = (f32[3,96,192]{2,1,0:T(8,128)S(1)}, f32[3,96,192]{2,1,0:T(8,128)}, u32[]{:S(2)}) copy-start(f32[3,96,192]{2,1,0:T(8,128)} %param.21) | copy-start | bytes 663556
  7.2 113.5 %all-gather.4.cloned.1.call-start = ((), (), s32[]{:S(2)}) async-start(), calls=%async_computation.7 | async-start | bytes 1966080 | tf_op jit(solution)/shard_map/all_gather | solution.py:63
  8.6 68.9 %copy-start = (bf16[2,256,768]{2,1,0:T(8,128)(2,1)S(1)}, bf16[2,256,768]{2,1,0:T(8,128)(2,1)}, u32[]{:S(2)}) copy-start(bf16[2,256,768]{2,1,0:T(8,128)(2,1)} %param.18) | copy-start | bytes 2359300
  10.2 68.8 %copy-start.39 = (f32[2,256]{1,0:T(2,128)}, f32[2,256]{1,0:T(2,128)S(1)}, u32[]{:S(2)}) copy-start(f32[2,256]{1,0:T(2,128)S(1)} %add_rsqrt_fusion) | copy-start | bytes 6148
  81.5 95.6 %all-gather.6.cloned.1.call-start = ((), (), s32[]{:S(2)}) async-start(), calls=%async_computation.8 | async-start | bytes 3096576 | tf_op jit(solution)/shard_map/all_gather | solution.py:55
  82.8 118.8 %reduce-scatter.12.cloned.1.call-start = ((), (), s32[]{:S(2)}) async-start(), calls=%async_computation.9 | async-start | bytes 983040 | tf_op jit(solution)/shard_map/reduce_scatter | solution.py:75
  82.9 40.7 %copy-start.27 = (bf16[2,256,3,64]{1,0,3,2:T(2,128)(2,1)}, bf16[2,256,3,64]{1,0,3,2:T(2,128)(2,1)S(1)}, u32[]{:S(2)}) copy-start(bf16[2,256,3,64]{1,0,3,2:T(2,128)(2,1)S(1)} %reshape_reshape.7) | copy-start | bytes 589828
  179.5 61.2 %reduce-scatter.16.cloned.1.call-start = ((), (), s32[]{:S(2)}) async-start(), calls=%async_computation.11 | async-start | bytes 983040 | tf_op jit(solution)/shard_map/reduce_scatter | solution.py:75
  216.9 49.5 %copy-start.33 = (f32[768]{0:T(1024)S(1)}, f32[768]{0:T(1024)}, u32[]{:S(2)}) copy-start(f32[768]{0:T(1024)} %get-tuple-element.141) | copy-start | bytes 9220
  216.9 49.5 %reduce-scatter.14.cloned.1.call-start = ((), (), s32[]{:S(2)}) async-start(), calls=%async_computation.10 | async-start | bytes 983040 | tf_op jit(solution)/shard_map/reduce_scatter | solution.py:75
  221.0 120.9 %reduce-scatter.18.cloned.1.call-start = ((), (), s32[]{:S(2)}) async-start(), calls=%async_computation.12 | async-start | bytes 1966080 | tf_op jit(solution)/shard_map/reduce_scatter | solution.py:67
  306.1 108.0 %reduce-scatter.24.cloned.1.call-start = ((), (), s32[]{:S(2)}) async-start(), calls=%async_computation.15 | async-start | bytes 2654208 | tf_op jit(solution)/shard_map/reduce_scatter | solution.py:59
  312.3 126.9 %reduce-scatter.20.cloned.1.call-start = ((), (), s32[]{:S(2)}) async-start(), calls=%async_computation.13 | async-start | bytes 983040 | tf_op jit(solution)/shard_map/reduce_scatter | solution.py:75
  329.8 13.2 %copy-start.2 = (bf16[768,576]{1,0:T(8,128)(2,1)S(1)}, bf16[768,576]{1,0:T(8,128)(2,1)}, u32[]{:S(2)}) copy-start(bf16[768,576]{1,0:T(8,128)(2,1)} %copy-done.1) | copy-start | bytes 2654212
  344.8 161.9 %reduce-scatter.22.cloned.1.call-start = ((), (), s32[]{:S(2)}) async-start(), calls=%async_computation.14 | async-start | bytes 1327104
  350.3 64.8 %copy-start.10 = (f32[768,96]{0,1:T(8,128)S(1)}, f32[768,96]{0,1:T(8,128)}, u32[]{:S(2)}) copy-start(f32[768,96]{0,1:T(8,128)} %param.30) | copy-start | bytes 884740
  352.6 64.8 %copy-start.12 = (f32[96,768]{1,0:T(8,128)S(1)}, f32[96,768]{1,0:T(8,128)}, u32[]{:S(2)}) copy-start(f32[96,768]{1,0:T(8,128)} %param.27) | copy-start | bytes 884740
  415.1 24.0 %copy-start.3 = (f32[2,256,768]{2,1,0:T(8,128)S(1)}, f32[2,256,768]{2,1,0:T(8,128)}, u32[]{:S(2)}) copy-start(f32[2,256,768]{2,1,0:T(8,128)} %get-tuple-element.122) | copy-start | bytes 4718596
  417.4 23.0 %copy-start.41 = (f32[1,768]{1,0:T(1,128)S(1)}, f32[1,768]{1,0:T(1,128)}, u32[]{:S(2)}) copy-start(f32[1,768]{1,0:T(1,128)} %stack.48) | copy-start | bytes 9220
  417.4 63.3 %copy-start.42 = (f32[12,96]{1,0:T(8,128)S(1)}, f32[12,96]{1,0:T(8,128)}, u32[]{:S(2)}) copy-start(f32[12,96]{1,0:T(8,128)} %param.34) | copy-start | bytes 13828
  417.4 63.3 %copy-start.43 = (f32[12,96]{1,0:T(8,128)S(1)}, f32[12,96]{1,0:T(8,128)}, u32[]{:S(2)}) copy-start(f32[12,96]{1,0:T(8,128)} %param.35) | copy-start | bytes 13828
  417.4 64.1 %copy-start.45 = (f32[2,64]{1,0:T(2,128)S(1)}, f32[2,64]{1,0:T(2,128)}, u32[]{:S(2)}) copy-start(f32[2,64]{1,0:T(2,128)} %constant_dynamic-slice_fusion) | copy-start | bytes 1540
  440.4 67.5 %copy-start.13 = (f32[3,96,192]{1,2,0:T(8,128)S(1)}, f32[3,96,192]{1,2,0:T(8,128)}, u32[]{:S(2)}) copy-start(f32[3,96,192]{1,2,0:T(8,128)} %copy.135) | copy-start | bytes 663556
  440.4 67.5 %copy-start.14 = (f32[3,96,192]{1,2,0:T(8,128)S(1)}, f32[3,96,192]{1,2,0:T(8,128)}, u32[]{:S(2)}) copy-start(f32[3,96,192]{1,2,0:T(8,128)} %copy.136) | copy-start | bytes 663556
  (38 other events, 101.9 us)
Sparse Core Ops, SparseCore 0:
  81.7 39.0 all-gather.3
  122.8 54.2 all-gather.5
  179.7 21.8 reduce-scatter.11
  217.0 23.6 reduce-scatter.15
  243.1 23.2 reduce-scatter.13
  306.2 35.6 reduce-scatter.17
  345.8 68.2 reduce-scatter.23
  416.8 22.3 reduce-scatter.19
  442.6 64.1 reduce-scatter.21

commit v2 on v1

--- a/solution.py
+++ b/solution.py
@@ -1,6 +1,8 @@
 import jax
 import jax.numpy as jnp
 from jax import lax
+from jax.experimental import pallas as pl
+from jax.experimental.pallas import tpu as pltpu
 from jax.sharding import PartitionSpec as P
 
 HD = 64
@@ -51,33 +53,412 @@
     return (weight - rate * (update + decay * weight), first_new, second_new)
 
 
-def gather_weights(shard):
-    return lax.all_gather(shard, ("dp", "ctx"), axis=0, tiled=True)
-
-
-def scatter_grads(grads):
-    return lax.psum_scatter(grads, ("dp", "ctx"), scatter_dimension=0, tiled=True)
-
-
-def gather_ctx(values):
-    return lax.all_gather(values, "ctx", axis=1, tiled=True)
-
-
-def scatter_ctx(values):
-    return lax.psum_scatter(values, "ctx", scatter_dimension=1, tiled=True)
-
-
-def gather_tensor(values):
-    return lax.all_gather(values, "tensor", axis=1, tiled=True)
-
-
-def scatter_tensor(values):
-    return lax.psum_scatter(values, "tensor", scatter_dimension=1, tiled=True)
-
-
-def my_rows(values):
-    part = values.shape[1] // lax.axis_size("tensor")
-    return lax.dynamic_slice_in_dim(values, lax.axis_index("tensor") * part, part, 1)
+def whole(count):
+    return [pl.BlockSpec(memory_space=pltpu.VMEM)] * count
+
+
+def params(number):
+    return pltpu.CompilerParams(
+        collective_id=number, has_side_effects=True, vmem_limit_bytes=48 * 2**20
+    )
+
+
+def place(axis, step):
+    size = lax.axis_size(axis)
+    return lax.rem(lax.axis_index(axis) + step + size, size)
+
+
+def push(source, target, sends, receives, device):
+    copy = pltpu.make_async_remote_copy(
+        src_ref=source,
+        dst_ref=target,
+        send_sem=sends,
+        recv_sem=receives,
+        device_id=device,
+        device_id_type=pl.DeviceIdType.MESH,
+    )
+    copy.start()
+    return copy
+
+
+def greet(axes):
+    barrier = pltpu.get_barrier_semaphore()
+    count = 0
+    for axis in axes:
+        for step in range(1, lax.axis_size(axis)):
+            pl.semaphore_signal(
+                barrier,
+                inc=1,
+                device_id={axis: place(axis, step)},
+                device_id_type=pl.DeviceIdType.MESH,
+            )
+            count += 1
+    pl.semaphore_wait(barrier, count)
+
+
+def weights_kernel(shard, small, out, small_out, zs, zr, xs, xr, szs, szr, sxs, sxr):
+    groups, rows = lax.axis_size("dp"), lax.axis_size("ctx")
+    me_dp, me_ctx = lax.axis_index("dp"), lax.axis_index("ctx")
+    greet(("dp", "ctx"))
+    waits = []
+    along = []
+    for source, target, sends, receives in ((small, small_out, szs, szr), (shard, out, zs, zr)):
+        for step in range(1, rows):
+            along.append(
+                push(
+                    source,
+                    target.at[me_dp, me_ctx],
+                    sends.at[step - 1],
+                    receives.at[step - 1],
+                    {"ctx": place("ctx", step)},
+                )
+            )
+    across = []
+    arrived = iter(along)
+    for source, target, sends, receives in ((small, small_out, sxs, sxr), (shard, out, xs, xr)):
+        target[me_dp, me_ctx] = source[...]
+        for step in range(rows):
+            owner = place("ctx", -step)
+            if step > 0:
+                next(arrived).wait_recv()
+            block = source if step == 0 else target.at[me_dp, owner]
+            for far in range(1, groups):
+                across.append(
+                    push(
+                        block,
+                        target.at[me_dp, owner],
+                        sends.at[step, far - 1],
+                        receives.at[step, far - 1],
+                        {"dp": place("dp", far)},
+                    )
+                )
+    for copy in across:
+        copy.wait_recv()
+    for copy in along + across:
+        copy.wait_send()
+
+
+def gather_weights(shard, small):
+    groups, rows = lax.axis_size("dp"), lax.axis_size("ctx")
+    dma = pltpu.SemaphoreType.DMA
+    one = [dma((max(rows - 1, 1),))] * 2 + [dma((rows, max(groups - 1, 1)))] * 2
+    return pl.pallas_call(
+        weights_kernel,
+        out_shape=(
+            jax.ShapeDtypeStruct((groups, rows) + shard.shape, shard.dtype),
+            jax.ShapeDtypeStruct((groups, rows) + small.shape, small.dtype),
+        ),
+        in_specs=whole(2),
+        out_specs=tuple(whole(2)),
+        scratch_shapes=one + one,
+        compiler_params=params(1),
+    )(shard, small)
+
+
+def gather_ctx_kernel(local, out, sends, receives):
+    rows, tokens = lax.axis_size("ctx"), local.shape[1]
+    start = pl.multiple_of(lax.axis_index("ctx") * tokens, tokens)
+    greet(("ctx",))
+    copies = [
+        push(
+            local,
+            out.at[:, pl.ds(start, tokens), :],
+            sends.at[step - 1],
+            receives.at[step - 1],
+            {"ctx": place("ctx", step)},
+        )
+        for step in range(1, rows)
+    ]
+    out[:, pl.ds(start, tokens), :] = local[...]
+    for copy in copies:
+        copy.wait()
+
+
+def gather_ctx(local):
+    rows = lax.axis_size("ctx")
+    batch, tokens, width = local.shape
+    return pl.pallas_call(
+        gather_ctx_kernel,
+        out_shape=jax.ShapeDtypeStruct((batch, rows * tokens, width), local.dtype),
+        in_specs=whole(1),
+        out_specs=whole(1)[0],
+        scratch_shapes=[pltpu.SemaphoreType.DMA((rows - 1,))] * 2,
+        compiler_params=params(2),
+    )(local)
+
+
+def scatter_ctx_kernel(parts, out, landing, sends, receives):
+    rows, tokens = lax.axis_size("ctx"), out.shape[1]
+    greet(("ctx",))
+    copies = []
+    for step in range(1, rows):
+        peer = place("ctx", step)
+        copies.append(
+            push(
+                parts.at[:, pl.ds(pl.multiple_of(peer * tokens, tokens), tokens), :],
+                landing.at[step - 1],
+                sends.at[step - 1],
+                receives.at[step - 1],
+                {"ctx": peer},
+            )
+        )
+    start = pl.multiple_of(lax.axis_index("ctx") * tokens, tokens)
+    for copy in copies:
+        copy.wait()
+    total = parts[:, pl.ds(start, tokens), :].astype(F32)
+    for step in range(1, rows):
+        total = total + landing[step - 1].astype(F32)
+    out[...] = total.astype(LOW)
+
+
+def scatter_ctx(parts):
+    rows = lax.axis_size("ctx")
+    batch, length, width = parts.shape
+    shape = (batch, length // rows, width)
+    return pl.pallas_call(
+        scatter_ctx_kernel,
+        out_shape=jax.ShapeDtypeStruct(shape, LOW),
+        in_specs=whole(1),
+        out_specs=whole(1)[0],
+        scratch_shapes=[pltpu.VMEM((rows - 1,) + shape, LOW)]
+        + [pltpu.SemaphoreType.DMA((rows - 1,))] * 2,
+        compiler_params=params(3),
+    )(parts)
+
+
+def start_shares(parts, landing, sends, receives):
+    share = landing.shape[2]
+    copies = []
+    for step in range(1, lax.axis_size("tensor")):
+        peer = place("tensor", step)
+        copies.append(
+            push(
+                parts.at[:, pl.ds(pl.multiple_of(peer * share, share), share), :],
+                landing.at[step - 1],
+                sends.at[step - 1],
+                receives.at[step - 1],
+                {"tensor": peer},
+            )
+        )
+    return copies
+
+
+def sum_shares(parts, landing, start):
+    total = parts[:, pl.ds(start, landing.shape[2]), :].astype(F32)
+    for step in range(landing.shape[0]):
+        total = total + landing[step].astype(F32)
+    return total
+
+
+def spread_shares(out, start, share, sends, receives):
+    copies = []
+    for step in range(1, lax.axis_size("tensor")):
+        mine = out.at[:, pl.ds(start, share), :]
+        copies.append(
+            push(
+                mine, mine, sends.at[step - 1], receives.at[step - 1], {"tensor": place("tensor", step)}
+            )
+        )
+    return copies
+
+
+def forward_share_kernel(parts, inputs, table, out, middle, landing, s0, r0, s1, r1):
+    share = middle.shape[1]
+    start = pl.multiple_of(lax.axis_index("tensor") * share, share)
+    greet(("tensor",))
+    copies = start_shares(parts, landing, s0, r0)
+    for copy in copies:
+        copy.wait()
+    total = sum_shares(parts, landing, start)
+    values = inputs[:, pl.ds(start, share), :].astype(F32) + total + table[4:5][None]
+    middle[...] = values
+    unit, scale = unit_norm(values)
+    out[:, pl.ds(start, share), :] = (unit * table[5:6][None] + table[6:7][None]).astype(LOW)
+    for copy in spread_shares(out, start, share, s1, r1):
+        copy.wait()
+
+
+def backward_share_kernel(parts, back, middle, table, out, grad, sums, landing, s0, r0, s1, r1):
+    share = middle.shape[1]
+    start = pl.multiple_of(lax.axis_index("tensor") * share, share)
+    greet(("tensor",))
+    copies = start_shares(parts, landing, s0, r0)
+    back_rows = back[:, pl.ds(start, share), :].astype(F32)
+    unit, scale = unit_norm(middle[...])
+    for copy in copies:
+        copy.wait()
+    total = sum_shares(parts, landing, start)
+    values = back_rows + norm_back(total, table[5:6][None], unit, scale)
+    grad[...] = values
+    out[:, pl.ds(start, share), :] = values.astype(LOW)
+    copies = spread_shares(out, start, share, s1, r1)
+    sums[...] = jnp.zeros_like(sums)
+    for row, term in enumerate((values, total * unit, total, back_rows)):
+        sums[row : row + 1] = jnp.sum(jnp.sum(term, axis=0), axis=0, keepdims=True)
+    for copy in copies:
+        copy.wait()
+
+
+def share_scratch(parts, copies):
+    ways = lax.axis_size("tensor")
+    batch, tokens, model = parts.shape
+    return [pltpu.VMEM((ways - 1, batch, tokens // ways, model), LOW)] + [
+        pltpu.SemaphoreType.DMA((ways - 1,))
+    ] * copies
+
+
+def forward_share(parts, inputs, table):
+    ways = lax.axis_size("tensor")
+    batch, tokens, model = parts.shape
+    return pl.pallas_call(
+        forward_share_kernel,
+        out_shape=(
+            jax.ShapeDtypeStruct(parts.shape, LOW),
+            jax.ShapeDtypeStruct((batch, tokens // ways, model), F32),
+        ),
+        in_specs=whole(3),
+        out_specs=tuple(whole(2)),
+        scratch_shapes=share_scratch(parts, 4),
+        compiler_params=params(4),
+    )(parts, inputs, table)
+
+
+def backward_share(parts, back, middle, table):
+    return pl.pallas_call(
+        backward_share_kernel,
+        out_shape=(
+            jax.ShapeDtypeStruct(parts.shape, LOW),
+            jax.ShapeDtypeStruct(middle.shape, F32),
+            jax.ShapeDtypeStruct((8, parts.shape[2]), F32),
+        ),
+        in_specs=whole(4),
+        out_specs=tuple(whole(3)),
+        scratch_shapes=share_scratch(parts, 4),
+        compiler_params=params(5),
+    )(parts, back, middle, table)
+
+
+def final_kernel(
+    grads, first_part, down_part, inputs, middle, middle_grad, table, owned,
+    grad_sum, input_grad, result, vector_sum,
+    land_dp, pass_on, land_ctx, land_first, land_down, land_t, land_c, land_d,
+    xs, xr, zs, zr, fs, fr, ds, dr, ts, tr, cs, cr, es, er,
+):
+    groups, rows = lax.axis_size("dp"), lax.axis_size("ctx")
+    me_dp, me_ctx = lax.axis_index("dp"), lax.axis_index("ctx")
+    share = middle.shape[1]
+    start = pl.multiple_of(lax.axis_index("tensor") * share, share)
+    greet(("dp", "ctx", "tensor"))
+    order = list(range(1, rows)) + [0]
+    across = {}
+    for step in order:
+        for far in range(1, groups):
+            peer = place("dp", far)
+            across[step, far] = push(
+                grads.at[peer, place("ctx", step)],
+                land_dp.at[step, far - 1],
+                xs.at[step, far - 1],
+                xr.at[step, far - 1],
+                {"dp": peer},
+            )
+    first_copies = start_shares(first_part, land_first, fs, fr)
+    down_copies = start_shares(down_part, land_down, ds, dr)
+
+    along = []
+    for step in order:
+        owner = place("ctx", step)
+        for far in range(1, groups):
+            across[step, far].wait()
+        total = grads[me_dp, owner].astype(F32)
+        for far in range(1, groups):
+            total = total + land_dp[step, far - 1].astype(F32)
+        if step == 0:
+            grad_sum[...] = total
+        else:
+            pass_on[step - 1] = total.astype(LOW)
+            along.append(
+                push(
+                    pass_on.at[step - 1],
+                    land_ctx.at[step - 1],
+                    zs.at[step - 1],
+                    zr.at[step - 1],
+                    {"ctx": owner},
+                )
+            )
+
+    for copy in first_copies:
+        copy.wait()
+    total = sum_shares(first_part, land_first, start)
+    unit, scale = unit_norm(inputs[:, pl.ds(start, share), :].astype(F32))
+    input_grad[...] = middle_grad[...] + norm_back(total, table[0:1][None], unit, scale)
+    vector_sum[...] = owned[...]
+    vector_sum[0:1] = jnp.sum(jnp.sum(total * unit, axis=0), axis=0, keepdims=True)
+    vector_sum[1:2] = jnp.sum(jnp.sum(total, axis=0), axis=0, keepdims=True)
+    for axis, land, sends, receives in (
+        ("tensor", land_t, ts, tr),
+        ("ctx", land_c, cs, cr),
+        ("dp", land_d, es, er),
+    ):
+        copies = [
+            push(
+                vector_sum,
+                land.at[step - 1],
+                sends.at[step - 1],
+                receives.at[step - 1],
+                {axis: place(axis, step)},
+            )
+            for step in range(1, lax.axis_size(axis))
+        ]
+        for copy in copies:
+            copy.wait()
+        summed = vector_sum[...]
+        for step in range(1, lax.axis_size(axis)):
+            summed = summed + land[step - 1]
+        vector_sum[...] = summed
+
+    for copy in down_copies:
+        copy.wait()
+    total = sum_shares(down_part, land_down, start)
+    result[...] = (middle[...] + total + table[7:8][None]).astype(LOW)
+    for copy in along:
+        copy.wait()
+    summed = grad_sum[...]
+    for step in range(1, rows):
+        summed = summed + land_ctx[step - 1].astype(F32)
+    grad_sum[...] = summed
+
+
+def finish(grads, first_part, down_part, inputs, middle, middle_grad, table, owned):
+    groups, rows = lax.axis_size("dp"), lax.axis_size("ctx")
+    ways = lax.axis_size("tensor")
+    block = grads.shape[2:]
+    dma = pltpu.SemaphoreType.DMA
+    land = pltpu.VMEM((ways - 1,) + middle.shape, LOW)
+    pairs = ((rows, groups - 1), (rows - 1,), (ways - 1,), (ways - 1,))
+    pairs += ((ways - 1,), (rows - 1,), (groups - 1,))
+    return pl.pallas_call(
+        final_kernel,
+        out_shape=(
+            jax.ShapeDtypeStruct(block, F32),
+            jax.ShapeDtypeStruct(middle.shape, F32),
+            jax.ShapeDtypeStruct(middle.shape, LOW),
+            jax.ShapeDtypeStruct(owned.shape, F32),
+        ),
+        in_specs=whole(8),
+        out_specs=tuple(whole(4)),
+        scratch_shapes=[
+            pltpu.VMEM((rows, groups - 1) + block, LOW),
+            pltpu.VMEM((rows - 1,) + block, LOW),
+            pltpu.VMEM((rows - 1,) + block, LOW),
+            land,
+            land,
+            pltpu.VMEM((ways - 1,) + owned.shape, F32),
+            pltpu.VMEM((rows - 1,) + owned.shape, F32),
+            pltpu.VMEM((groups - 1,) + owned.shape, F32),
+        ]
+        + [dma(shape) for shape in pairs for _ in range(2)],
+        compiler_params=params(6),
+    )(grads, first_part, down_part, inputs, middle, middle_grad, table, owned)
 
 
 def allowed_pairs(segment, tokens):
@@ -153,28 +534,32 @@
     rows_all = batch * tokens
     tensor_index = lax.axis_index("tensor")
 
-    attn_shard = jnp.concatenate(
-        [qkv_weight[0], qkv_weight[1], qkv_weight[2]], axis=1
+    shard = jnp.concatenate(
+        [qkv_weight[0], qkv_weight[1], qkv_weight[2], out_weight.T, up_weight, down_weight.T],
+        axis=1,
     ).astype(LOW)
-    rest_shard = jnp.concatenate([out_weight.T, up_weight, down_weight.T], axis=1).astype(LOW)
-    table = lax.all_gather(
-        vectors.astype(LOW), ("dp", "ctx"), axis=1, tiled=True
-    ).astype(F32)
-    proj = gather_weights(attn_shard)
-    rest = gather_weights(rest_shard)
-    out_turned = rest[:, :width]
-    up = rest[:, width : width + units]
-    down_turned = rest[:, width + units :]
-
-    inputs = hidden_in.astype(F32)
-    unit_first, scale_first = unit_norm(inputs)
+    table_rows, part = vectors.shape
+    pad_rows = -table_rows % 16
+    small = jnp.pad(vectors.astype(LOW), ((0, pad_rows), (0, -part % 128)))
+    gathered, small_all = gather_weights(shard, small)
+    gathered = gathered.reshape(model, shard.shape[1])
+    small_all = small_all.reshape((-1,) + small.shape)[:, :, :part]
+    table = small_all.transpose(1, 0, 2).reshape(small.shape[0], model).astype(F32)
+    proj = gathered[:, : 3 * width]
+    out_turned = gathered[:, 3 * width : 4 * width]
+    up = gathered[:, 4 * width : 4 * width + units]
+    down_turned = gathered[:, 4 * width + units :]
+
+    unit_first, _ = unit_norm(hidden_in.astype(F32))
     first_norm = (unit_first * table[0] + table[1]).astype(LOW).reshape(rows_all, model)
     projected = dot(first_norm, proj, 1, 0)
     query_bias = lax.dynamic_slice_in_dim(table[2], tensor_index * width, width)
     value_bias = lax.dynamic_slice_in_dim(table[3], tensor_index * width, width)
     query = (projected[:, :width] + query_bias).astype(LOW).reshape(batch, tokens, width)
     local_kv = (
-        jnp.concatenate([projected[:, width : 2 * width], projected[:, 2 * width :] + value_bias], axis=1)
+        jnp.concatenate(
+            [projected[:, width : 2 * width], projected[:, 2 * width :] + value_bias], axis=1
+        )
         .astype(LOW)
         .reshape(batch, tokens, 2 * width)
     )
@@ -185,29 +570,25 @@
     mixed = mixed.reshape(rows_all, width)
 
     attn_part = dot(mixed, out_turned, 1, 1).astype(LOW).reshape(batch, tokens, model)
-    middle = my_rows(inputs) + scatter_tensor(attn_part).astype(F32) + table[4]
-    unit_second, scale_second = unit_norm(middle)
-    second_norm = gather_tensor((unit_second * table[5] + table[6]).astype(LOW))
+    second_norm, middle = forward_share(attn_part, hidden_in, table)
     second_norm = second_norm.reshape(rows_all, model)
-    unit_bias = lax.dynamic_slice_in_dim(table[8:].reshape(-1), tensor_index * units, units)
+    unit_bias = lax.dynamic_slice_in_dim(
+        table[8:table_rows].reshape(-1), tensor_index * units, units
+    )
     hidden = dot(second_norm, up, 1, 0) + unit_bias
     gelu_value, gelu_pull = jax.vjp(jax.nn.gelu, hidden)
     active = gelu_value.astype(LOW)
     down_part = dot(active, down_turned, 1, 1).astype(LOW).reshape(batch, tokens, model)
-    result = (middle + scatter_tensor(down_part).astype(F32) + table[7]).astype(LOW)
 
     back = cotangent.reshape(rows_all, model)
-    back_rows = my_rows(cotangent).astype(F32)
     hidden_grad = gelu_pull(dot(back, down_turned, 1, 0))[0]
     hidden_low = hidden_grad.astype(LOW)
     second_part = dot(hidden_low, up, 1, 1).astype(LOW).reshape(batch, tokens, model)
-    second_grad = scatter_tensor(second_part).astype(F32)
+    middle_low, middle_grad, late_rows = backward_share(second_part, cotangent, middle, table)
     grad_down = dot(back, active, 0, 0)
     grad_up = dot(second_norm, hidden_low, 0, 0)
-    late_sum = scatter_grads(jnp.concatenate([grad_up, grad_down], axis=1).astype(LOW))
-
-    middle_grad = back_rows + norm_back(second_grad, table[5], unit_second, scale_second)
-    middle_low = gather_tensor(middle_grad.astype(LOW)).reshape(rows_all, model)
+
+    middle_low = middle_low.reshape(rows_all, model)
     mixed_grad = dot(middle_low, out_turned, 1, 0).astype(LOW).reshape(batch, tokens, width)
     query_grad, key_part, value_part = attend_back(mixed_grad, query, keys, values, probs)
     kv_grad = scatter_ctx(jnp.concatenate([key_part, value_part], axis=2).astype(LOW))
@@ -216,47 +597,35 @@
         rows_all, 3 * width
     )
     first_part = dot(stacked, proj, 1, 1).astype(LOW).reshape(batch, tokens, model)
-    first_grad = scatter_tensor(first_part).astype(F32)
     grad_qkv = dot(first_norm, stacked, 0, 0)
-    early_sum = scatter_grads(jnp.concatenate([grad_qkv, grad_out], axis=1).astype(LOW))
-    my_unit, my_scale = my_rows(unit_first), my_rows(scale_first)
-    input_grad = middle_grad + norm_back(first_grad, table[0], my_unit, my_scale)
-
-    def total(values):
-        return jnp.sum(values, axis=(0, 1))
-
-    owned = jnp.zeros((vectors.shape[0] * model,), F32)
+    grads = jnp.concatenate([grad_qkv, grad_out, grad_up, grad_down], axis=1).astype(LOW)
+    grads = grads.reshape((lax.axis_size("dp"), lax.axis_size("ctx")) + shard.shape)
+
+    owned = jnp.zeros((small.shape[0] * model,), F32)
     owned = lax.dynamic_update_slice(
-        owned, total(query_grad), (2 * model + tensor_index * width,)
+        owned, jnp.sum(query_grad, axis=(0, 1)), (2 * model + tensor_index * width,)
     )
     owned = lax.dynamic_update_slice(
-        owned, total(value_part), (3 * model + tensor_index * width,)
-    )
+        owned, jnp.sum(value_part, axis=(0, 1)), (3 * model + tensor_index * width,)
+    )
+    owned = lax.dynamic_update_slice(owned, late_rows[:4].reshape(-1), (4 * model,))
     owned = lax.dynamic_update_slice(
         owned, jnp.sum(hidden_grad, axis=0), (8 * model + tensor_index * units,)
-    )
-    zero = jnp.zeros((model,), F32)
-    rows = jnp.stack(
-        [total(first_grad * my_unit), total(first_grad), zero, zero]
-        + [total(middle_grad), total(second_grad * unit_second)]
-        + [total(second_grad), total(back_rows)]
-        + [zero] * (vectors.shape[0] - 8)
-    )
-    grad_table = lax.psum(owned.reshape(rows.shape) + rows, ("dp", "ctx", "tensor"))
-    part = vectors.shape[1]
+    ).reshape(small.shape[0], model)
+
+    grad_sum, input_grad, result, vector_sum = finish(
+        grads, first_part, down_part, hidden_in, middle, middle_grad, table, owned
+    )
     grad_vectors = lax.dynamic_slice_in_dim(
-        grad_table,
+        vector_sum[:table_rows],
         (lax.axis_index("dp") * lax.axis_size("ctx") + lax.axis_index("ctx")) * part,
         part,
         1,
     )
-
-    early_sum = early_sum.astype(F32)
-    late_sum = late_sum.astype(F32)
-    qkv_sum = jnp.stack([early_sum[:, place * width : (place + 1) * width] for place in range(3)])
-    out_sum = early_sum[:, 3 * width :].T
-    up_sum = late_sum[:, :units]
-    down_sum = late_sum[:, units:].T
+    qkv_sum = jnp.stack([grad_sum[:, at * width : (at + 1) * width] for at in range(3)])
+    out_sum = grad_sum[:, 3 * width : 4 * width].T
+    up_sum = grad_sum[:, 4 * width : 4 * width + units]
+    down_sum = grad_sum[:, 4 * width + units :].T
     return (
         result,
         input_grad,

time: 519 us -> 371 us (0.71)
  waiting for transfers between devices: 262 us -> 0 us
  Pallas kernels: 0 us -> 242 us
  blocking collectives: 123 us -> 0 us
  local copies, waits for them, and re-layouts: 22.5 us -> 38.4 us
  between operations: 14.7 us -> 1.35 us
  other arithmetic: 25.3 us -> 12.1 us
  matrix products: 69.9 us -> 76.5 us
    pallas_call x0 -> x6, Pallas kernels: none -> 242 us  [the longest x1 70.3 us: finish(): pl.pallas_call(final_kernel, out_shape=(jax.ShapeDtypeStruct(block, F32),...]
    reduce_scatter x6 -> x0, waiting for transfers between devices: 158 us -> none  [the longest x4 85.1 us: scatter_tensor(): return lax.psum_scatter(values, 'tensor', scatter_dimension=1, tiled=True)]
    all_gather x4 -> x0, blocking collectives: 82.9 us -> none  [the longest x1 34.2 us: gather_weights(): return lax.all_gather(shard, ('dp', 'ctx'), axis=0, tiled=True)]
    all_gather x2 -> x0, waiting for transfers between devices: 80.6 us -> none  [the longest x1 43.4 us: gather_weights(): return lax.all_gather(shard, ('dp', 'ctx'), axis=0, tiled=True)]
    psum x1 -> x0, blocking collectives: 40.2 us -> none  [on_device(): lax.psum(owned.reshape(rows.shape) + rows, ('dp', 'ctx', 'tensor'))]
    unnamed x10 -> x0, waiting for transfers between devices: 23.7 us -> none
    concatenate x3 -> x2, local copies, waits for them, and re-layouts: 1.11 us -> 6.64 us  [the longest x1 6.53 us: on_device(): jnp.concatenate([grad_qkv, grad_out, grad_up, grad_down], axis=1)]
    reduce_sum x4 -> x1, other arithmetic: 5.54 us -> 0.16 us  [on_device(): jnp.sum(value_part, axis=(0, 1))]
  transfers between devices with their start and end apart: 9 -> 0, of which waited for: 9 -> 0; matrix products, arithmetic and copies ran while one was open for 12% -> 0% of each run, Pallas kernels for 0% -> 0%
where the time goes in v2:
time: 371 us; the launch traced here: 370 us
  Pallas kernels  242 us (65%)
  matrix products  76.5 us (21%)
  local copies, waits for them, and re-layouts  38.4 us (10%)
  other arithmetic  12.1 us (3%)
    pallas_call x1, Pallas kernels, finish(): pl.pallas_call(final_kernel, out_shape=(jax.ShapeDtypeStruct(block, F32),...  70.3 us
    pallas_call x1, Pallas kernels, gather_weights(): pl.pallas_call(weights_kernel, out_shape=(jax.ShapeDtypeStruct((groups, r...  56.4 us
    pallas_call x1, Pallas kernels, scatter_ctx(): pl.pallas_call(scatter_ctx_kernel, out_shape=jax.ShapeDtypeStruct(shape,...  38.3 us
    pallas_call x1, Pallas kernels, gather_ctx(): pl.pallas_call(gather_ctx_kernel, out_shape=jax.ShapeDtypeStruct((batch,...  35.7 us
    dot_general x12, matrix products, dot(): lax.dot_general(left, right, (((left_dim,), (right_dim,)), ((), ())), pre...  21.2 us
    pallas_call x1, Pallas kernels, backward_share(): pl.pallas_call(backward_share_kernel, out_shape=(jax.ShapeDtypeStruct(par...  20.8 us
    pallas_call x1, Pallas kernels, forward_share(): pl.pallas_call(forward_share_kernel, out_shape=(jax.ShapeDtypeStruct(part...  20.4 us
    dot_general x1, matrix products, attend_back(): jnp.einsum('bhqk,bqhd->bkhd', score_grad, heads_of(query), preferred_elem...  17.9 us

profile of v2, /device:TPU:0, one launch (start us, length us, event | category | flops | bytes accessed | tf_op | source)
XLA Modules:
  0.0 370.1 jit_solution(12801799691561584683)
XLA Ops:
  7.8 56.4 %shard_map.305 = (bf16[2,4,96,2304]{3,2,1,0:T(8,128)(2,1)S(1)}, bf16[2,4,16,128]{3,2,1,0:T(8,128)(2,1)S(1)}) custom-call(bf16[96,2304]{1,0:T(8,128)(2,1)S(1)} %concatenate.29.shard, bf16[16,128]{1,0:T(8,128)(2,1)S(1)} %pad.4.small), custom_call_target="tpu_custom_call" | custom-call | tf_op jit(solution)/shard_map/pallas_call | solution.py:145
  64.2 1.7 copy-done.1
  66.9 2.2 fusion.50
  70.4 35.7 %shard_map.306 = bf16[2,1024,384]{2,1,0:T(8,128)(2,1)S(1)} custom-call(bf16[2,256,384]{2,1,0:T(8,128)(2,1)S(1)} %pad_maximum_fusion.2.local), custom_call_target="tpu_custom_call" | custom-call | tf_op jit(solution)/shard_map/pallas_call | solution.py:180
  108.9 6.2 %fusion.97 = (f32[2,3,256]{2,1,0:T(4,128)S(1)}, f32[2,3,256,1024]{3,2,1,0:T(8,128)}) fusion(pred[2,256,1024]{2,1,0:T(8,128)(4,1)} %compare_and_fusion, bf16[2,1024,3,64]{1,3,2,0:T(8,128)(2,1)S(1)} %bitcast.154, bf16[2,256,3,64]{1,0,3,2:T(2,128)(2,1)} %reshape_reshape.7), kind=kOutput, calls=%fused_computation.137 | convolution fusion | flops 207619072 | bytes 7804928 | tf_op jit(solution)/shard_map/sub | solution.py:484
  115.2 3.9 %fusion.42 = bf16[2,3,64,256]{3,2,1,0:T(8,128)(2,1)S(1)} fusion(bf16[2,1024,3,64]{1,3,2,0:T(8,128)(2,1)S(1)} %bitcast.146, f32[2,3,256,1024]{3,2,1,0:T(8,128)} %get-tuple-element.105, f32[2,3,256]{2,1,0:T(4,128)S(1)} %get-tuple-element.104), kind=kOutput, calls=%fused_computation.56 | convolution fusion | flops 204570624 | bytes 7280640 | tf_op jit(solution)/shard_map/bhqk,bkhd->bqhd/dot_general | solution.py:486
  121.0 20.4 %shard_map.307 = (bf16[2,256,768]{2,1,0:T(8,128)(2,1)S(1)}, f32[2,64,768]{2,1,0:T(8,128)S(1)}) custom-call(bf16[2,256,768]{2,1,0:T(8,128)(2,1)S(1)} %bitcast.127, bf16[2,256,768]{2,1,0:T(8,128)(2,1)S(1)} %copy-done, f32[16,768]{1,0:T(8,128)S(1)} %convert_element_type.86.table), custom_call_target="tpu_custom_call" | custom-call | tf_op jit(solution)/shard_map/pallas_call | solution.py:313
  141.7 2.2 convolution_add_fusion
  146.7 2.1 convolution_convert_fusion
  148.8 1.8 convolution_convert_fusion.1
  151.4 20.8 %shard_map.308 = (bf16[2,256,768]{2,1,0:T(8,128)(2,1)S(1)}, f32[2,64,768]{2,1,0:T(8,128)S(1)}, f32[8,768]{1,0:T(8,128)S(1)}) custom-call(bf16[2,256,768]{2,1,0:T(8,128)(2,1)S(1)} %bitcast.142, bf16[2,256,768]{2,1,0:T(8,128)(2,1)S(1)} %copy-done.4, f32[2,64,768]{2,1,0:T(8,128)S(1)} %get-tuple-element.31.middle, f32[16,768]{1,0:T(8,128)S(1)} %convert_element_type.86.table), custom_call_target="tpu_custom_call" | custom-call | tf_op jit(solution)/shard_map/pallas_call | solution.py:327
  172.3 1.6 convolution_convert_fusion.6
  178.2 4.7 %bitcast_convert_fusion.1 = (bf16[2,1024,3,64]{1,3,2,0:T(8,128)(2,1)}, f32[2,3,64,1024]{3,2,1,0:T(8,128)S(1)}) fusion(f32[2,3,256,1024]{3,2,1,0:T(8,128)} %get-tuple-element.105, f32[2,3,256]{2,1,0:T(4,128)S(1)} %get-tuple-element.104, bf16[2,256,3,64]{1,0,3,2:T(2,128)(2,1)S(1)} %copy-done.21), kind=kOutput, calls=%fused_computation.36 | convolution fusion | flops 204865536 | bytes 8853504 | tf_op jit(solution)/shard_map/bhqk,bqhd->bkhd/dot_general | solution.py:505
  184.5 4.9 %fusion.68 = f32[2,3,256,1024]{3,2,1,0:T(8,128)} fusion(bf16[2,1024,3,64]{1,3,2,0:T(8,128)(2,1)} %bitcast.147, bf16[2,256,3,64]{1,0,3,2:T(2,128)(2,1)} %reshape_reshape.8), kind=kOutput, calls=%fused_computation.97 | convolution fusion | flops 201326592 | bytes 7274496 | tf_op jit(solution)/shard_map/bqhd,bkhd->bhqk/dot_general | solution.py:494
  189.4 17.6 %fusion.95 = (f32[3,64]{1,0:T(4,128)S(1)}, bf16[2,256,3,64]{1,3,2,0:T(8,128)(2,1)}) fusion(bf16[2,1024,3,64]{1,3,2,0:T(8,128)(2,1)} %bitcast.153, f32[2,3,256,1024]{3,2,1,0:T(8,128)} %fusion.68, f32[2,3,256,1024]{3,2,1,0:T(8,128)} %get-tuple-element.105, f32[2,3,256]{2,1,0:T(4,128)S(1)} %get-tuple-element.104), kind=kOutput, calls=%fused_computation.135 | convolution fusion | flops 212535616 | bytes 13572864 | tf_op jit(solution)/shard_map/bhqk,bkhd->bqhd/dot_general | solution.py:499
  207.0 17.9 %fusion.36 = bf16[2,3,64,1024]{3,2,1,0:T(8,128)(2,1)} fusion(f32[2,3,256,1024]{3,2,1,0:T(8,128)} %fusion.68, bf16[2,256,3,64]{1,0,3,2:T(2,128)(2,1)} %reshape_reshape.7, f32[2,3,256,1024]{3,2,1,0:T(8,128)} %get-tuple-element.105, f32[2,3,256]{2,1,0:T(4,128)S(1)} %get-tuple-element.104), kind=kOutput, calls=%fused_computation.54 | convolution fusion | flops 212732416 | bytes 13572096 | tf_op jit(solution)/shard_map/bhqk,bqhd->bkhd/dot_general | solution.py:502
  231.4 1.8 copy.74
  233.2 2.2 copy.72
  235.4 1.8 pad_maximum_fusion.parts
  237.2 38.3 %shard_map.309 = bf16[2,256,384]{2,1,0:T(8,128)(2,1)S(1)} custom-call(bf16[2,1024,384]{2,1,0:T(8,128)(2,1)S(1)} %pad_maximum_fusion.parts), custom_call_target="tpu_custom_call" | custom-call | tf_op jit(solution)/shard_map/pallas_call | solution.py:218
  275.6 1.8 bitcast_convert_fusion
  277.7 2.9 convolution_convert_fusion.4
  282.1 6.5 %concatenate.37.grads = bf16[2,4,96,2304]{3,2,1,0:T(8,128)(2,1)} concatenate(bf16[2,4,96,576]{3,2,1,0:T(8,128)(2,1)S(1)} %bitcast.145, bf16[2,4,96,192]{3,2,1,0:T(8,128)(2,1)} %bitcast.149, bf16[2,4,96,768]{3,2,1,0:T(8,128)(2,1)} %convolution_convert_fusion.1, bf16[2,4,96,768]{3,2,1,0:T(8,128)(2,1)} %bitcast.150), dimensions={3} | concatenate | bytes 7077888 | tf_op jit(solution)/shard_map/concatenate | solution.py:601
  289.8 70.3 %shard_map.310 = (f32[96,2304]{1,0:T(8,128)S(1)}, f32[2,64,768]{2,1,0:T(8,128)S(1)}, bf16[2,64,768]{2,1,0:T(8,128)(2,1)S(1)}, f32[16,768]{1,0:T(8,128)S(1)}) custom-call(bf16[2,4,96,2304]{3,2,1,0:T(8,128)(2,1)} %concatenate.37.grads, bf16[2,256,768]{2,1,0:T(8,128)(2,1)S(1)} %bitcast.137, bf16[2,256,768]{2,1,0:T(8,128)(2,1)S(1)} %bitcast.136, ...), custom_call_target="tpu_custom_call" | custom-call | tf_op jit(solution)/shard_map/pallas_call | solution.py:439
  (151 shorter events, 43.0 us)
Async XLA Ops:
  0.7 3.7 %copy-start.35 = (f32[12,96]{1,0:T(8,128)S(1)}, f32[12,96]{1,0:T(8,128)}, u32[]{:S(2)}) copy-start(f32[12,96]{1,0:T(8,128)} %param.33) | copy-start | bytes 13828
  0.7 5.4 %copy-start.11 = (f32[3,96,192]{2,1,0:T(8,128)S(1)}, f32[3,96,192]{2,1,0:T(8,128)}, u32[]{:S(2)}) copy-start(f32[3,96,192]{2,1,0:T(8,128)} %param.21) | copy-start | bytes 663556
  0.7 4.7 %copy-start.34 = (f32[192,96]{1,0:T(8,128)S(1)}, f32[192,96]{1,0:T(8,128)}, u32[]{:S(2)}) copy-start(f32[192,96]{1,0:T(8,128)} %param.26) | copy-start | bytes 221188
  0.7 3.9 %copy-start.33 = (f32[192,96]{1,0:T(8,128)S(1)}, f32[192,96]{1,0:T(8,128)}, u32[]{:S(2)}) copy-start(f32[192,96]{1,0:T(8,128)} %param.25) | copy-start | bytes 221188
  0.7 3.7 %copy-start.32 = (f32[192,96]{1,0:T(8,128)S(1)}, f32[192,96]{1,0:T(8,128)}, u32[]{:S(2)}) copy-start(f32[192,96]{1,0:T(8,128)} %param.24) | copy-start | bytes 221188
  0.7 5.4 %copy-start.15 = (f32[96,768]{1,0:T(8,128)S(1)}, f32[96,768]{1,0:T(8,128)}, u32[]{:S(2)}) copy-start(f32[96,768]{1,0:T(8,128)} %param.27) | copy-start | bytes 884740
  1.5 4.6 %copy-start.13 = (f32[768,96]{0,1:T(8,128)S(1)}, f32[768,96]{0,1:T(8,128)}, u32[]{:S(2)}) copy-start(f32[768,96]{0,1:T(8,128)} %param.30) | copy-start | bytes 884740
  6.2 60.4 %copy-start = (bf16[2,256,768]{2,1,0:T(8,128)(2,1)S(1)}, bf16[2,256,768]{2,1,0:T(8,128)(2,1)}, u32[]{:S(2)}) copy-start(bf16[2,256,768]{2,1,0:T(8,128)(2,1)} %inputs.3) | copy-start | bytes 2359300
  66.9 2.2 copy-start.9
  108.5 6.7 %copy-start.8 = (bf16[2,1024,192]{1,2,0:T(8,128)(2,1)}, bf16[2,1024,192]{1,2,0:T(8,128)(2,1)S(1)}, u32[]{:S(2)}) copy-start(bf16[2,1024,192]{1,2,0:T(8,128)(2,1)S(1)} %copy.67) | copy-start | bytes 2359300
  141.6 2.4 copy-start.2
  175.8 2.3 copy-start.21
  237.2 38.3 %copy-start.10 = (bf16[2,256,768]{2,1,0:T(8,128)(2,1)S(1)}, bf16[2,256,768]{2,1,0:T(8,128)(2,1)}, u32[]{:S(2)}) copy-start(bf16[2,256,768]{2,1,0:T(8,128)(2,1)} %copy-done.9) | copy-start | bytes 2359300
  237.2 38.3 %copy-start.17 = (bf16[2,256,192]{2,1,0:T(8,128)(2,1)S(1)}, bf16[2,256,192]{2,1,0:T(8,128)(2,1)}, u32[]{:S(2)}) copy-start(bf16[2,256,192]{2,1,0:T(8,128)(2,1)} %copy.74) | copy-start | bytes 589828
  289.8 71.7 %copy-start.19 = (f32[192,96]{0,1:T(8,128)S(1)}, f32[192,96]{0,1:T(8,128)}, u32[]{:S(2)}) copy-start(f32[192,96]{0,1:T(8,128)} %copy-done.18) | copy-start | bytes 221188
  289.8 71.7 %copy-start.22 = (f32[192,96]{0,1:T(8,128)S(1)}, f32[192,96]{0,1:T(8,128)}, u32[]{:S(2)}) copy-start(f32[192,96]{0,1:T(8,128)} %copy.80) | copy-start | bytes 221188
  289.8 71.7 %copy-start.23 = (f32[192,96]{0,1:T(8,128)S(1)}, f32[192,96]{0,1:T(8,128)}, u32[]{:S(2)}) copy-start(f32[192,96]{0,1:T(8,128)} %copy.81) | copy-start | bytes 221188
  289.8 72.6 %copy-start.37 = (f32[12,96]{1,0:T(8,128)S(1)}, f32[12,96]{1,0:T(8,128)}, u32[]{:S(2)}) copy-start(f32[12,96]{1,0:T(8,128)} %param.34) | copy-start | bytes 13828
  361.5 4.0 %copy-start.12 = (f32[3,96,192]{2,1,0:T(8,128)S(1)}, f32[3,96,192]{2,1,0:T(8,128)}, u32[]{:S(2)}) copy-start(f32[3,96,192]{2,1,0:T(8,128)} %param.21) | copy-start | bytes 663556
  361.5 4.0 %copy-start.24 = (f32[3,96,192]{2,1,0:T(8,128)S(1)}, f32[3,96,192]{2,1,0:T(8,128)}, u32[]{:S(2)}) copy-start(f32[3,96,192]{2,1,0:T(8,128)} %param.22) | copy-start | bytes 663556
  361.5 4.0 %copy-start.25 = (f32[3,96,192]{2,1,0:T(8,128)S(1)}, f32[3,96,192]{2,1,0:T(8,128)}, u32[]{:S(2)}) copy-start(f32[3,96,192]{2,1,0:T(8,128)} %param.23) | copy-start | bytes 663556
  362.4 4.2 %copy-start.14 = (f32[768,96]{0,1:T(8,128)S(1)}, f32[768,96]{0,1:T(8,128)}, u32[]{:S(2)}) copy-start(f32[768,96]{0,1:T(8,128)} %param.30) | copy-start | bytes 884740
  362.4 4.2 %copy-start.26 = (f32[768,96]{0,1:T(8,128)S(1)}, f32[768,96]{0,1:T(8,128)}, u32[]{:S(2)}) copy-start(f32[768,96]{0,1:T(8,128)} %param.31) | copy-start | bytes 884740
  362.4 4.2 %copy-start.27 = (f32[768,96]{0,1:T(8,128)S(1)}, f32[768,96]{0,1:T(8,128)}, u32[]{:S(2)}) copy-start(f32[768,96]{0,1:T(8,128)} %param.32) | copy-start | bytes 884740
  (14 other events, 21.2 us)

commit v3 on v2

--- a/solution.py
+++ b/solution.py
@@ -1,3 +1,5 @@
+import functools
+
 import jax
 import jax.numpy as jnp
 from jax import lax
@@ -155,75 +157,254 @@
     )(shard, small)
 
 
-def gather_ctx_kernel(local, out, sends, receives):
-    rows, tokens = lax.axis_size("ctx"), local.shape[1]
-    start = pl.multiple_of(lax.axis_index("ctx") * tokens, tokens)
-    greet(("ctx",))
-    copies = [
+def head_lanes(width, offset, head):
+    lanes = lax.broadcasted_iota(jnp.int32, (1, width), 1) - offset
+    return ((lanes >= head * HD) & (lanes < (head + 1) * HD)).astype(F32)
+
+
+def softmax_of(query, keys, allowed):
+    scores = dot(query, keys, 1, 1) * HD ** (-0.5)
+    scores = jnp.where(allowed, scores, -1e30)
+    weights = jnp.exp(scores - jnp.max(scores, axis=-1, keepdims=True))
+    return weights * (1.0 / jnp.sum(weights, axis=-1, keepdims=True))
+
+
+def allowed_pairs(segment_row, segment_column):
+    tokens, length = segment_column.shape[0], segment_row.shape[1]
+    first = lax.axis_index("ctx") * tokens
+    queries = first + lax.broadcasted_iota(jnp.int32, (tokens, length), 0)
+    keys = lax.broadcasted_iota(jnp.int32, (tokens, length), 1)
+    return (queries >= keys) & (segment_column == segment_row)
+
+
+def attend_kernel(
+    width, local, query, segment_row, segment_column, shard,
+    all_kv, mixed, out,
+    total, ks, kr, zs, zr, xs, xr,
+):
+    groups, rows = lax.axis_size("dp"), lax.axis_size("ctx")
+    me_dp, me_ctx = lax.axis_index("dp"), lax.axis_index("ctx")
+    batch, tokens = local.shape[:2]
+    key_width, value_width = query.shape[2], mixed.shape[2]
+    lead = 2 * width - value_width
+    start = pl.multiple_of(me_ctx * tokens, tokens)
+    greet(("dp", "ctx"))
+    kv_copies = [
         push(
             local,
-            out.at[:, pl.ds(start, tokens), :],
-            sends.at[step - 1],
-            receives.at[step - 1],
+            all_kv.at[:, pl.ds(start, tokens), :],
+            ks.at[step - 1],
+            kr.at[step - 1],
             {"ctx": place("ctx", step)},
         )
         for step in range(1, rows)
     ]
-    out[:, pl.ds(start, tokens), :] = local[...]
-    for copy in copies:
-        copy.wait()
-
-
-def gather_ctx(local):
-    rows = lax.axis_size("ctx")
-    batch, tokens, width = local.shape
+    along = [
+        push(
+            shard,
+            out.at[me_dp, me_ctx],
+            zs.at[step - 1],
+            zr.at[step - 1],
+            {"ctx": place("ctx", step)},
+        )
+        for step in range(1, rows)
+    ]
+    across = []
+
+    def send_across(step):
+        owner = place("ctx", -step)
+        block = shard if step == 0 else out.at[me_dp, owner]
+        for far in range(1, groups):
+            across.append(
+                push(
+                    block,
+                    out.at[me_dp, owner],
+                    xs.at[step, far - 1],
+                    xr.at[step, far - 1],
+                    {"dp": place("dp", far)},
+                )
+            )
+
+    send_across(0)
+    all_kv[:, pl.ds(start, tokens), :] = local[...]
+    out[me_dp, me_ctx] = shard[...]
+    for copy in kv_copies:
+        copy.wait()
+    for one in range(batch):
+        allowed = allowed_pairs(segment_row[one], segment_column[one])
+        total[...] = jnp.zeros_like(total)
+
+        def one_head(head, carry):
+            masked = query[one] * head_lanes(key_width, 0, head).astype(LOW)
+            probs = softmax_of(masked, all_kv[one, :, :key_width], allowed)
+            part = dot(probs.astype(LOW), all_kv[one, :, lead:], 1, 0)
+            total[...] += part * head_lanes(value_width, width - lead, head)
+            return carry
+
+        lax.fori_loop(0, width // HD, one_head, 0)
+        mixed[one] = total[...].astype(LOW)
+        if one == 0:
+            for step in range(1, rows):
+                along[step - 1].wait_recv()
+                send_across(step)
+    for copy in across:
+        copy.wait_recv()
+    for copy in along + across:
+        copy.wait_send()
+
+
+def attend(width, local, query, segment_row, segment_column, shard):
+    groups, rows = lax.axis_size("dp"), lax.axis_size("ctx")
+    batch, tokens = local.shape[:2]
+    value_width = 2 * width - width // 128 * 128
+    dma = pltpu.SemaphoreType.DMA
     return pl.pallas_call(
-        gather_ctx_kernel,
-        out_shape=jax.ShapeDtypeStruct((batch, rows * tokens, width), local.dtype),
-        in_specs=whole(1),
-        out_specs=whole(1)[0],
-        scratch_shapes=[pltpu.SemaphoreType.DMA((rows - 1,))] * 2,
+        functools.partial(attend_kernel, width),
+        out_shape=(
+            jax.ShapeDtypeStruct((batch, rows * tokens, 2 * width), LOW),
+            jax.ShapeDtypeStruct((batch, tokens, value_width), LOW),
+            jax.ShapeDtypeStruct((groups, rows) + shard.shape, LOW),
+        ),
+        in_specs=whole(5),
+        out_specs=tuple(whole(3)),
+        scratch_shapes=[pltpu.VMEM((tokens, value_width), F32)]
+        + [dma((rows - 1,))] * 4
+        + [dma((rows, groups - 1))] * 2,
         compiler_params=params(2),
-    )(local)
-
-
-def scatter_ctx_kernel(parts, out, landing, sends, receives):
-    rows, tokens = lax.axis_size("ctx"), out.shape[1]
-    greet(("ctx",))
-    copies = []
+    )(local, query, segment_row, segment_column, shard)
+
+
+def attend_back_kernel(
+    width, mixed_grad, query, all_kv, segment_row, segment_column, g0, g1, g2,
+    kv_grad, query_grad, value_sum, sum0, sum1, sum2,
+    total, parts, landing, dp0, dp1, dp2, pass0, pass1, pass2, ctx0, ctx1, ctx2,
+    ks, kr, xs, xr, zs, zr,
+):
+    groups, rows = lax.axis_size("dp"), lax.axis_size("ctx")
+    me_dp, me_ctx = lax.axis_index("dp"), lax.axis_index("ctx")
+    batch, tokens = kv_grad.shape[:2]
+    key_width, value_width = query.shape[2], mixed_grad.shape[2]
+    lead = 2 * width - value_width
+    weights = (
+        (g0, sum0, dp0, pass0, ctx0),
+        (g1, sum1, dp1, pass1, ctx1),
+        (g2, sum2, dp2, pass2, ctx2),
+    )
+    order = list(range(1, rows)) + [0]
+    greet(("dp", "ctx"))
+    across, along = {}, []
+    for step in order:
+        for at, (grads, _, land_dp, _, _) in enumerate(weights):
+            for far in range(1, groups):
+                peer = place("dp", far)
+                across[step, at, far] = push(
+                    grads.at[peer, place("ctx", step)],
+                    land_dp.at[step, far - 1],
+                    xs.at[at, step, far - 1],
+                    xr.at[at, step, far - 1],
+                    {"dp": peer},
+                )
+    value_sum[...] = jnp.zeros_like(value_sum)
+    kv_copies = []
+    for one in range(batch):
+        allowed = allowed_pairs(segment_row[one], segment_column[one])
+        total[...] = jnp.zeros_like(total)
+        query_grad[one] = jnp.zeros(query_grad.shape[1:], F32)
+
+        def one_head(head, carry):
+            lanes = head_lanes(key_width, 0, head)
+            masked = query[one] * lanes.astype(LOW)
+            keys = all_kv[one, :, :key_width]
+            probs = softmax_of(masked, keys, allowed)
+            masked_grad = mixed_grad[one] * head_lanes(value_width, width - lead, head).astype(LOW)
+            prob_grad = dot(masked_grad, all_kv[one, :, lead:], 1, 1)
+            delta = jnp.sum(prob_grad * probs, axis=-1, keepdims=True)
+            score_grad = (probs * (prob_grad - delta) * HD ** (-0.5)).astype(LOW)
+            query_grad[one] += dot(score_grad, keys, 1, 0) * lanes
+            total[:, :key_width] += dot(score_grad, masked, 0, 0)
+            total[:, lead:] += dot(probs.astype(LOW), masked_grad, 0, 0)
+            return carry
+
+        lax.fori_loop(0, width // HD, one_head, 0)
+        value_sum[0:1] += jnp.sum(total[...], axis=0, keepdims=True)
+        parts[one] = total[...].astype(LOW)
+        for step in range(1, rows):
+            peer = place("ctx", step)
+            kv_copies.append(
+                push(
+                    parts.at[one, pl.ds(pl.multiple_of(peer * tokens, tokens), tokens), :],
+                    landing.at[step - 1, one],
+                    ks.at[one, step - 1],
+                    kr.at[one, step - 1],
+                    {"ctx": peer},
+                )
+            )
+        if one == 0:
+            for step in order:
+                owner = place("ctx", step)
+                for at, (grads, summed, land_dp, pass_on, land_ctx) in enumerate(weights):
+                    for far in range(1, groups):
+                        across[step, at, far].wait()
+                    value = grads[me_dp, owner].astype(F32)
+                    for far in range(1, groups):
+                        value = value + land_dp[step, far - 1].astype(F32)
+                    if step == 0:
+                        summed[...] = value
+                    else:
+                        pass_on[step - 1] = value.astype(LOW)
+                        along.append(
+                            push(
+                                pass_on.at[step - 1],
+                                land_ctx.at[step - 1],
+                                zs.at[at, step - 1],
+                                zr.at[at, step - 1],
+                                {"ctx": owner},
+                            )
+                        )
+    start = pl.multiple_of(me_ctx * tokens, tokens)
+    for copy in kv_copies:
+        copy.wait()
+    value = parts[:, pl.ds(start, tokens), :].astype(F32)
     for step in range(1, rows):
-        peer = place("ctx", step)
-        copies.append(
-            push(
-                parts.at[:, pl.ds(pl.multiple_of(peer * tokens, tokens), tokens), :],
-                landing.at[step - 1],
-                sends.at[step - 1],
-                receives.at[step - 1],
-                {"ctx": peer},
-            )
+        value = value + landing[step - 1].astype(F32)
+    kv_grad[...] = value.astype(LOW)
+    for copy in along:
+        copy.wait()
+    for _, summed, _, _, land_ctx in weights:
+        value = summed[...]
+        for step in range(1, rows):
+            value = value + land_ctx[step - 1].astype(F32)
+        summed[...] = value
+
+
+def attend_back(width, mixed_grad, query, all_kv, segment_row, segment_column, weight_grads):
+    groups, rows = lax.axis_size("dp"), lax.axis_size("ctx")
+    batch, tokens, key_width = query.shape
+    length = rows * tokens
+    blocks = [grads.shape[2:] for grads in weight_grads]
+    dma = pltpu.SemaphoreType.DMA
+    return pl.pallas_call(
+        functools.partial(attend_back_kernel, width),
+        out_shape=(
+            jax.ShapeDtypeStruct((batch, tokens, 2 * width), LOW),
+            jax.ShapeDtypeStruct(query.shape, F32),
+            jax.ShapeDtypeStruct((8, 2 * width), F32),
         )
-    start = pl.multiple_of(lax.axis_index("ctx") * tokens, tokens)
-    for copy in copies:
-        copy.wait()
-    total = parts[:, pl.ds(start, tokens), :].astype(F32)
-    for step in range(1, rows):
-        total = total + landing[step - 1].astype(F32)
-    out[...] = total.astype(LOW)
-
-
-def scatter_ctx(parts):
-    rows = lax.axis_size("ctx")
-    batch, length, width = parts.shape
-    shape = (batch, length // rows, width)
-    return pl.pallas_call(
-        scatter_ctx_kernel,
-        out_shape=jax.ShapeDtypeStruct(shape, LOW),
-        in_specs=whole(1),
-        out_specs=whole(1)[0],
-        scratch_shapes=[pltpu.VMEM((rows - 1,) + shape, LOW)]
-        + [pltpu.SemaphoreType.DMA((rows - 1,))] * 2,
+        + tuple(jax.ShapeDtypeStruct(block, F32) for block in blocks),
+        in_specs=whole(8),
+        out_specs=tuple(whole(6)),
+        scratch_shapes=[
+            pltpu.VMEM((length, 2 * width), F32),
+            pltpu.VMEM((batch, length, 2 * width), LOW),
+            pltpu.VMEM((rows - 1, batch, tokens, 2 * width), LOW),
+        ]
+        + [pltpu.VMEM((rows, groups - 1) + block, LOW) for block in blocks]
+        + [pltpu.VMEM((rows - 1,) + block, LOW) for block in blocks] * 2
+        + [dma((batch, rows - 1))] * 2
+        + [dma((3, rows, groups - 1))] * 2
+        + [dma((3, rows - 1))] * 2,
         compiler_params=params(3),
-    )(parts)
+    )(mixed_grad, query, all_kv, segment_row, segment_column, *weight_grads)
 
 
 def start_shares(parts, landing, sends, receives):
@@ -461,53 +642,6 @@
     )(grads, first_part, down_part, inputs, middle, middle_grad, table, owned)
 
 
-def allowed_pairs(segment, tokens):
-    ctx_index = lax.axis_index("ctx")
-    key_places = jnp.arange(segment.shape[1], dtype=jnp.int32)
-    query_places = ctx_index * tokens + jnp.arange(tokens, dtype=jnp.int32)
-    query_segment = lax.dynamic_slice_in_dim(segment, ctx_index * tokens, tokens, 1)
-    return (query_places[None, :, None] >= key_places[None, None, :]) & (
-        query_segment[:, :, None] == segment[:, None, :]
-    )
-
-
-def heads_of(values):
-    batch, tokens, width = values.shape
-    return values.reshape(batch, tokens, width // HD, HD)
-
-
-def attend(query, keys, values, allowed):
-    scores = jnp.einsum(
-        "bqhd,bkhd->bhqk", heads_of(query), heads_of(keys), preferred_element_type=F32
-    ) * HD ** (-0.5)
-    scores = jnp.where(allowed[:, None], scores, -1e30)
-    weights = jnp.exp(scores - jnp.max(scores, axis=-1, keepdims=True))
-    probs = weights / jnp.sum(weights, axis=-1, keepdims=True)
-    mixed = jnp.einsum(
-        "bhqk,bkhd->bqhd", probs.astype(LOW), heads_of(values), preferred_element_type=F32
-    )
-    return mixed.reshape(query.shape).astype(LOW), probs
-
-
-def attend_back(mixed_grad, query, keys, values, probs):
-    grad_heads = heads_of(mixed_grad)
-    prob_grad = jnp.einsum(
-        "bqhd,bkhd->bhqk", grad_heads, heads_of(values), preferred_element_type=F32
-    )
-    row_delta = jnp.sum(prob_grad * probs, axis=-1, keepdims=True)
-    score_grad = (probs * (prob_grad - row_delta) * HD ** (-0.5)).astype(LOW)
-    query_grad = jnp.einsum(
-        "bhqk,bkhd->bqhd", score_grad, heads_of(keys), preferred_element_type=F32
-    ).reshape(query.shape)
-    key_grad = jnp.einsum(
-        "bhqk,bqhd->bkhd", score_grad, heads_of(query), preferred_element_type=F32
-    ).reshape(keys.shape)
-    value_grad = jnp.einsum(
-        "bhqk,bqhd->bkhd", probs.astype(LOW), grad_heads, preferred_element_type=F32
-    ).reshape(keys.shape)
-    return query_grad, key_grad, value_grad
-
-
 def on_device(
     hidden_in,
     cotangent,
@@ -534,21 +668,15 @@
     rows_all = batch * tokens
     tensor_index = lax.axis_index("tensor")
 
-    shard = jnp.concatenate(
-        [qkv_weight[0], qkv_weight[1], qkv_weight[2], out_weight.T, up_weight, down_weight.T],
-        axis=1,
-    ).astype(LOW)
+    shard = jnp.concatenate([qkv_weight[0], qkv_weight[1], qkv_weight[2]], axis=1).astype(LOW)
+    rest_shard = jnp.concatenate([up_weight, down_weight.T, out_weight.T], axis=1).astype(LOW)
     table_rows, part = vectors.shape
     pad_rows = -table_rows % 16
     small = jnp.pad(vectors.astype(LOW), ((0, pad_rows), (0, -part % 128)))
     gathered, small_all = gather_weights(shard, small)
-    gathered = gathered.reshape(model, shard.shape[1])
+    proj = gathered.reshape(model, shard.shape[1])
     small_all = small_all.reshape((-1,) + small.shape)[:, :, :part]
     table = small_all.transpose(1, 0, 2).reshape(small.shape[0], model).astype(F32)
-    proj = gathered[:, : 3 * width]
-    out_turned = gathered[:, 3 * width : 4 * width]
-    up = gathered[:, 4 * width : 4 * width + units]
-    down_turned = gathered[:, 4 * width + units :]
 
     unit_first, _ = unit_norm(hidden_in.astype(F32))
     first_norm = (unit_first * table[0] + table[1]).astype(LOW).reshape(rows_all, model)
@@ -563,11 +691,18 @@
         .astype(LOW)
         .reshape(batch, tokens, 2 * width)
     )
-    all_kv = gather_ctx(local_kv)
-    keys, values = all_kv[..., :width], all_kv[..., width:]
-    allowed = allowed_pairs(segment_ids, tokens)
-    mixed, probs = attend(query, keys, values, allowed)
-    mixed = mixed.reshape(rows_all, width)
+    lead = width // 128 * 128
+    query = jnp.pad(query, ((0, 0), (0, 0), (0, -width % 128)))
+    segment_row = segment_ids[:, None, :]
+    segment_column = lax.dynamic_slice_in_dim(
+        segment_ids, lax.axis_index("ctx") * tokens, tokens, 1
+    )[:, :, None]
+    all_kv, mixed, rest = attend(width, local_kv, query, segment_row, segment_column, rest_shard)
+    rest = rest.reshape(model, rest_shard.shape[1])
+    up = rest[:, :units]
+    down_turned = rest[:, units : 2 * units]
+    out_turned = rest[:, 2 * units :]
+    mixed = mixed[:, :, width - lead :].reshape(rows_all, width)
 
     attn_part = dot(mixed, out_turned, 1, 1).astype(LOW).reshape(batch, tokens, model)
     second_norm, middle = forward_share(attn_part, hidden_in, table)
@@ -590,23 +725,29 @@
 
     middle_low = middle_low.reshape(rows_all, model)
     mixed_grad = dot(middle_low, out_turned, 1, 0).astype(LOW).reshape(batch, tokens, width)
-    query_grad, key_part, value_part = attend_back(mixed_grad, query, keys, values, probs)
-    kv_grad = scatter_ctx(jnp.concatenate([key_part, value_part], axis=2).astype(LOW))
+    mixed_grad = jnp.pad(mixed_grad, ((0, 0), (0, 0), (width - lead, 0)))
     grad_out = dot(middle_low, mixed, 0, 0)
+    blocks = (lax.axis_size("dp"), lax.axis_size("ctx"), shard.shape[0])
+    weight_grads = [
+        grads.astype(LOW).reshape(blocks + (-1,)) for grads in (grad_up, grad_down, grad_out)
+    ]
+    kv_grad, query_grad, value_sum, up_sum, down_sum, out_sum = attend_back(
+        width, mixed_grad, query, all_kv, segment_row, segment_column, weight_grads
+    )
+    query_grad = query_grad[:, :, :width]
     stacked = jnp.concatenate([query_grad.astype(LOW), kv_grad], axis=2).reshape(
         rows_all, 3 * width
     )
     first_part = dot(stacked, proj, 1, 1).astype(LOW).reshape(batch, tokens, model)
     grad_qkv = dot(first_norm, stacked, 0, 0)
-    grads = jnp.concatenate([grad_qkv, grad_out, grad_up, grad_down], axis=1).astype(LOW)
-    grads = grads.reshape((lax.axis_size("dp"), lax.axis_size("ctx")) + shard.shape)
+    grads = grad_qkv.astype(LOW).reshape(blocks + (-1,))
 
     owned = jnp.zeros((small.shape[0] * model,), F32)
     owned = lax.dynamic_update_slice(
         owned, jnp.sum(query_grad, axis=(0, 1)), (2 * model + tensor_index * width,)
     )
     owned = lax.dynamic_update_slice(
-        owned, jnp.sum(value_part, axis=(0, 1)), (3 * model + tensor_index * width,)
+        owned, value_sum[0, width:], (3 * model + tensor_index * width,)
     )
     owned = lax.dynamic_update_slice(owned, late_rows[:4].reshape(-1), (4 * model,))
     owned = lax.dynamic_update_slice(
@@ -623,9 +764,8 @@
         1,
     )
     qkv_sum = jnp.stack([grad_sum[:, at * width : (at + 1) * width] for at in range(3)])
-    out_sum = grad_sum[:, 3 * width : 4 * width].T
-    up_sum = grad_sum[:, 4 * width : 4 * width + units]
-    down_sum = grad_sum[:, 4 * width + units :].T
+    out_sum = out_sum.T
+    down_sum = down_sum.T
     return (
         result,
         input_grad,

time: 371 us -> 299 us (0.81)
  matrix products: 76.5 us -> 16.5 us
  local copies, waits for them, and re-layouts: 38.4 us -> 21.5 us
  Pallas kernels: 242 us -> 249 us
    pallas_call x2, Pallas kernels: 74 us -> 151 us  [the longest x1 76.5 us: attend_back(): pl.pallas_call(functools.partial(attend_back_kernel, width), out_shape=(j...]
    dot_general x5 -> x0, matrix products: 49 us -> none  [the longest x1 17.9 us: attend_back(): jnp.einsum('bhqk,bqhd->bkhd', score_grad, heads_of(query), preferred_elem...]
    pallas_call x1, Pallas kernels: 70.3 us -> 34.6 us  [finish(): pl.pallas_call(final_kernel, out_shape=(jax.ShapeDtypeStruct(block, F32),...]
    pallas_call x1, Pallas kernels: 56.4 us -> 22.2 us  [gather_weights(): pl.pallas_call(weights_kernel, out_shape=(jax.ShapeDtypeStruct((groups, r...]
    concatenate x2 -> x0, local copies, waits for them, and re-layouts: 6.64 us -> none  [the longest x1 6.53 us: on_device(): jnp.concatenate([grad_qkv, grad_out, grad_up, grad_down], axis=1)]
    sub x1 -> x0, matrix products: 6.2 us -> none  [attend(): weights = jnp.exp(scores - jnp.max(scores, axis=-1, keepdims=True))]
    unnamed x85 -> x80, local copies, waits for them, and re-layouts: 10.2 us -> 15.4 us
    dot_general x12, matrix products: 21.2 us -> 16.5 us  [dot(): lax.dot_general(left, right, (((left_dim,), (right_dim,)), ((), ())), pre...]
where the time goes in v3:
time: 299 us
  Pallas kernels  249 us (83%)
  local copies, waits for them, and re-layouts  21.5 us (7%)
  matrix products  16.5 us (6%)
  other arithmetic  9.94 us (3%)
    pallas_call x1, Pallas kernels, attend_back(): pl.pallas_call(functools.partial(attend_back_kernel, width), out_shape=(j...  76.5 us
    pallas_call x1, Pallas kernels, attend(): pl.pallas_call(functools.partial(attend_kernel, width), out_shape=(jax.Sh...  75 us
    pallas_call x1, Pallas kernels, finish(): pl.pallas_call(final_kernel, out_shape=(jax.ShapeDtypeStruct(block, F32),...  34.6 us
    pallas_call x1, Pallas kernels, gather_weights(): pl.pallas_call(weights_kernel, out_shape=(jax.ShapeDtypeStruct((groups, r...  22.2 us
    pallas_call x1, Pallas kernels, backward_share(): pl.pallas_call(backward_share_kernel, out_shape=(jax.ShapeDtypeStruct(par...  20.8 us
    pallas_call x1, Pallas kernels, forward_share(): pl.pallas_call(forward_share_kernel, out_shape=(jax.ShapeDtypeStruct(part...  20.4 us
    dot_general x12, matrix products, dot(): lax.dot_general(left, right, (((left_dim,), (right_dim,)), ((), ())), pre...  16.5 us
    unnamed x80, local copies, waits for them, and re-layouts  15.4 us

profile of v3, /device:TPU:0, one launch (start us, length us, event | category | flops | bytes accessed | tf_op | source)
XLA Modules:
  0.0 298.6 jit_solution(3516554046539921200)
XLA Ops:
  1.5 1.4 convert_reduce_fusion
  2.9 1.5 fusion.2
  6.5 22.2 %shard_map.305 = (bf16[2,4,96,576]{3,2,1,0:T(8,128)(2,1)S(1)}, bf16[2,4,16,128]{3,2,1,0:T(8,128)(2,1)S(1)}) custom-call(bf16[96,576]{1,0:T(8,128)(2,1)S(1)} %pad_maximum_fusion.4.shard, bf16[16,128]{1,0:T(8,128)(2,1)S(1)} %pad.12.small), custom_call_target="tpu_custom_call" | custom-call | tf_op jit(solution)/shard_map/pallas_call | solution.py:147
  31.3 75.0 %shard_map.306 = (bf16[2,1024,384]{2,1,0:T(8,128)(2,1)S(1)}, bf16[2,256,256]{2,1,0:T(8,128)(2,1)S(1)}, bf16[2,4,96,1728]{3,2,1,0:T(8,128)(2,1)S(1)}) custom-call(bf16[2,256,384]{2,1,0:T(8,128)(2,1)S(1)} %pad_maximum_fusion.1.local, bf16[2,256,256]{2,1,0:T(8,128)(2,1)S(1)} %pad.13.query, s32[2,1,1024]{2,1,0:T(1,128)S(1)} %broadcast_in_dim.6.segment_row, ...), custom_call_target="tpu_custom_call" | custom-call | tf_op jit(solution)/shard_map/pallas_call | solution.py:261
  106.3 1.2 copy-done.1
  108.1 20.4 %shard_map.307 = (bf16[2,256,768]{2,1,0:T(8,128)(2,1)S(1)}, f32[2,64,768]{2,1,0:T(8,128)S(1)}) custom-call(bf16[2,256,768]{2,1,0:T(8,128)(2,1)S(1)} %bitcast.96, bf16[2,256,768]{2,1,0:T(8,128)(2,1)S(1)} %copy-done, f32[16,768]{1,0:T(8,128)S(1)} %convert_element_type.75.table), custom_call_target="tpu_custom_call" | custom-call | tf_op jit(solution)/shard_map/pallas_call | solution.py:494
  129.2 2.0 convolution_convert_fusion.2
  131.2 1.5 fusion.42
  132.8 2.1 convolution_convert_fusion
  134.8 1.8 convolution_convert_fusion.1
  137.5 20.8 %shard_map.308 = (bf16[2,256,768]{2,1,0:T(8,128)(2,1)S(1)}, f32[2,64,768]{2,1,0:T(8,128)S(1)}, f32[8,768]{1,0:T(8,128)S(1)}) custom-call(bf16[2,256,768]{2,1,0:T(8,128)(2,1)S(1)} %bitcast.107, bf16[2,256,768]{2,1,0:T(8,128)(2,1)S(1)} %copy-done.8, f32[2,64,768]{2,1,0:T(8,128)S(1)} %get-tuple-element.42.middle, f32[16,768]{1,0:T(8,128)S(1)} %convert_element_type.75.table), custom_call_target="tpu_custom_call" | custom-call | tf_op jit(solution)/shard_map/pallas_call | solution.py:508
  158.8 1.2 fusion.15
  160.3 1.1 copy.60
  161.4 1.3 copy-done.2
  162.7 1.3 copy-done.3
  164.0 76.5 %shard_map.309 = (bf16[2,256,384]{2,1,0:T(8,128)(2,1)S(1)}, f32[2,256,256]{2,1,0:T(8,128)S(1)}, f32[8,384]{1,0:T(8,128)S(1)}, f32[96,768]{1,0:T(8,128)S(1)}, f32...) custom-call(bf16[2,256,256]{2,1,0:T(8,128)(2,1)S(1)} %pad.14.mixed_grad, bf16[2,256,256]{2,1,0:T(8,128)(2,1)S(1)} %pad.13.query, ...), custom_call_target="tpu_custom_call" | custom-call | tf_op jit(solution)/shard_map/pallas_call | solution.py:386
  245.2 3.1 %bitcast_convert_fusion = bf16[768,576]{0,1:T(8,128)(2,1)} fusion(bf16[2,256,768]{2,1,0:T(8,128)(2,1)} %copy-done.15, bf16[2,256,384]{2,1,0:T(8,128)(2,1)S(1)} %copy-done.10, bf16[2,256,192]{2,1,0:T(8,128)(2,1)S(1)} %slice.151), kind=kOutput, calls=%fused_computation.6 | convolution fusion | flops 454606848 | bytes 2260992 | tf_op jit(solution)/shard_map/dot_general | solution.py:29
  248.5 1.7 convolution_convert_fusion.4
  250.2 1.5 copy.63
  252.9 1.1 copy-done.7
  254.1 34.6 %shard_map.310 = (f32[96,576]{1,0:T(8,128)S(1)}, f32[2,64,768]{2,1,0:T(8,128)S(1)}, bf16[2,64,768]{2,1,0:T(8,128)(2,1)S(1)}, f32[16,768]{1,0:T(8,128)S(1)}) custom-call(bf16[2,4,96,576]{3,2,1,0:T(8,128)(2,1)S(1)} %bitcast.95, bf16[2,256,768]{2,1,0:T(8,128)(2,1)S(1)} %bitcast.104, bf16[2,256,768]{2,1,0:T(8,128)(2,1)S(1)} %bitcast.103, ...), custom_call_target="tpu_custom_call" | custom-call | tf_op jit(solution)/shard_map/pallas_call | solution.py:620
  289.4 1.6 copy.69
  291.0 1.6 copy.70
  292.8 2.3 multiply_subtract_fusion.2
  (132 shorter events, 18.6 us)
Async XLA Ops:
  0.7 3.8 %copy-start.32 = (f32[12,96]{1,0:T(8,128)S(1)}, f32[12,96]{1,0:T(8,128)}, u32[]{:S(2)}) copy-start(f32[12,96]{1,0:T(8,128)} %param.33) | copy-start | bytes 13828
  0.7 5.4 %copy-start.16 = (f32[3,96,192]{2,1,0:T(8,128)S(1)}, f32[3,96,192]{2,1,0:T(8,128)}, u32[]{:S(2)}) copy-start(f32[3,96,192]{2,1,0:T(8,128)} %param.21) | copy-start | bytes 663556
  0.7 3.8 %copy-start.33 = (s32[2,1024]{1,0:T(2,128)S(1)}, s32[2,1024]{1,0:T(2,128)}, u32[]{:S(2)}) copy-start(s32[2,1024]{1,0:T(2,128)} %param.20) | copy-start | bytes 24580
  0.7 4.7 %copy-start.31 = (f32[192,96]{1,0:T(8,128)S(1)}, f32[192,96]{1,0:T(8,128)}, u32[]{:S(2)}) copy-start(f32[192,96]{1,0:T(8,128)} %param.26) | copy-start | bytes 221188
  0.7 3.9 %copy-start.30 = (f32[192,96]{1,0:T(8,128)S(1)}, f32[192,96]{1,0:T(8,128)}, u32[]{:S(2)}) copy-start(f32[192,96]{1,0:T(8,128)} %param.25) | copy-start | bytes 221188
  0.7 3.8 %copy-start.29 = (f32[192,96]{1,0:T(8,128)S(1)}, f32[192,96]{1,0:T(8,128)}, u32[]{:S(2)}) copy-start(f32[192,96]{1,0:T(8,128)} %param.24) | copy-start | bytes 221188
  1.5 4.8 %copy-start.17 = (f32[96,768]{1,0:T(8,128)S(1)}, f32[96,768]{1,0:T(8,128)}, u32[]{:S(2)}) copy-start(f32[96,768]{1,0:T(8,128)} %param.27) | copy-start | bytes 884740
  2.9 3.4 %copy-start.19 = (f32[768,96]{0,1:T(8,128)S(1)}, f32[768,96]{0,1:T(8,128)}, u32[]{:S(2)}) copy-start(f32[768,96]{0,1:T(8,128)} %param.30) | copy-start | bytes 884740
  6.1 23.2 %copy-start = (bf16[2,256,768]{2,1,0:T(8,128)(2,1)S(1)}, bf16[2,256,768]{2,1,0:T(8,128)(2,1)}, u32[]{:S(2)}) copy-start(bf16[2,256,768]{2,1,0:T(8,128)(2,1)} %inputs.3) | copy-start | bytes 2359300
  164.0 78.7 %copy-start.22 = (f32[192,96]{0,1:T(8,128)S(1)}, f32[192,96]{0,1:T(8,128)}, u32[]{:S(2)}) copy-start(f32[192,96]{0,1:T(8,128)} %copy-done.21) | copy-start | bytes 221188
  164.0 78.7 %copy-start.23 = (f32[192,96]{0,1:T(8,128)S(1)}, f32[192,96]{0,1:T(8,128)}, u32[]{:S(2)}) copy-start(f32[192,96]{0,1:T(8,128)} %copy.64) | copy-start | bytes 221188
  164.0 78.7 %copy-start.24 = (f32[192,96]{0,1:T(8,128)S(1)}, f32[192,96]{0,1:T(8,128)}, u32[]{:S(2)}) copy-start(f32[192,96]{0,1:T(8,128)} %copy.65) | copy-start | bytes 221188
  242.6 2.5 copy-start.10
  245.1 3.4 %copy-start.5 = (bf16[2,4,96,576]{3,2,1,0:T(8,128)(2,1)S(1)}, bf16[2,4,96,576]{3,2,1,0:T(8,128)(2,1)}, u32[]{:S(2)}) copy-start(bf16[2,4,96,576]{3,2,1,0:T(8,128)(2,1)} %copy-done.4) | copy-start | bytes 2654212
  254.1 34.6 %copy-start.34 = (f32[12,96]{1,0:T(8,128)S(1)}, f32[12,96]{1,0:T(8,128)}, u32[]{:S(2)}) copy-start(f32[12,96]{1,0:T(8,128)} %param.34) | copy-start | bytes 13828
  254.1 34.6 %copy-start.35 = (f32[12,96]{1,0:T(8,128)S(1)}, f32[12,96]{1,0:T(8,128)}, u32[]{:S(2)}) copy-start(f32[12,96]{1,0:T(8,128)} %param.35) | copy-start | bytes 13828
  288.6 6.5 %copy-start.14 = (f32[96,768]{1,0:T(8,128)S(1)}, f32[96,768]{1,0:T(8,128)}, u32[]{:S(2)}) copy-start(f32[96,768]{1,0:T(8,128)} %copy-done.13) | copy-start | bytes 884740
  288.6 6.5 %copy-start.18 = (f32[96,768]{1,0:T(8,128)S(1)}, f32[96,768]{1,0:T(8,128)}, u32[]{:S(2)}) copy-start(f32[96,768]{1,0:T(8,128)} %param.27) | copy-start | bytes 884740
  288.6 6.4 %copy-start.25 = (f32[96,768]{1,0:T(8,128)S(1)}, f32[96,768]{1,0:T(8,128)}, u32[]{:S(2)}) copy-start(f32[96,768]{1,0:T(8,128)} %param.28) | copy-start | bytes 884740
  288.7 6.4 %copy-start.26 = (f32[96,768]{1,0:T(8,128)S(1)}, f32[96,768]{1,0:T(8,128)}, u32[]{:S(2)}) copy-start(f32[96,768]{1,0:T(8,128)} %param.29) | copy-start | bytes 884740
  292.7 3.4 %copy-start.12 = (f32[96,768]{1,0:T(8,128)S(1)}, f32[96,768]{1,0:T(8,128)}, u32[]{:S(2)}) copy-start(f32[96,768]{1,0:T(8,128)} %copy-done.11) | copy-start | bytes 884740
  292.8 3.4 %copy-start.20 = (f32[768,96]{0,1:T(8,128)S(1)}, f32[768,96]{0,1:T(8,128)}, u32[]{:S(2)}) copy-start(f32[768,96]{0,1:T(8,128)} %param.30) | copy-start | bytes 884740
  292.8 3.4 %copy-start.27 = (f32[768,96]{0,1:T(8,128)S(1)}, f32[768,96]{0,1:T(8,128)}, u32[]{:S(2)}) copy-start(f32[768,96]{0,1:T(8,128)} %param.31) | copy-start | bytes 884740
  292.8 3.4 %copy-start.28 = (f32[768,96]{0,1:T(8,128)S(1)}, f32[768,96]{0,1:T(8,128)}, u32[]{:S(2)}) copy-start(f32[768,96]{0,1:T(8,128)} %param.32) | copy-start | bytes 884740
  (12 other events, 13.5 us)

commit v4 on v3

--- a/solution.py
+++ b/solution.py
@@ -180,7 +180,7 @@
 def attend_kernel(
     width, local, query, segment_row, segment_column, shard,
     all_kv, mixed, out,
-    total, ks, kr, zs, zr, xs, xr,
+    total, ks, kr, zs, zr, ys, yr, xs, xr,
 ):
     groups, rows = lax.axis_size("dp"), lax.axis_size("ctx")
     me_dp, me_ctx = lax.axis_index("dp"), lax.axis_index("ctx")
@@ -189,47 +189,82 @@
     lead = 2 * width - value_width
     start = pl.multiple_of(me_ctx * tokens, tokens)
     greet(("dp", "ctx"))
-    kv_copies = [
-        push(
-            local,
-            all_kv.at[:, pl.ds(start, tokens), :],
-            ks.at[step - 1],
-            kr.at[step - 1],
-            {"ctx": place("ctx", step)},
+    def hop(source, target, step, sign, sends, receives):
+        owner = me_ctx - sign * step
+        far = me_ctx + sign
+        came = me_ctx - sign * (step + 1)
+        copy = pltpu.make_async_remote_copy(
+            src_ref=source if step == 0 else target(owner),
+            dst_ref=target(owner),
+            send_sem=sends.at[step],
+            recv_sem=receives.at[step],
+            device_id={"ctx": far},
+            device_id_type=pl.DeviceIdType.MESH,
         )
-        for step in range(1, rows)
+        sent = (owner >= 0) & (owner < rows) & (far >= 0) & (far < rows)
+        return copy, sent, (came >= 0) & (came < rows), came
+
+    def kv_at(owner):
+        return all_kv.at[:, pl.ds(pl.multiple_of(owner * tokens, tokens), tokens), :]
+
+    def block_at(owner):
+        return out.at[me_dp, owner]
+
+    kv_hops = [hop(local, kv_at, step, 1, ks, kr) for step in range(rows - 1)]
+    hops = [
+        (hop(shard, block_at, step, 1, zs, zr), hop(shard, block_at, step, -1, ys, yr))
+        for step in range(rows - 1)
     ]
-    along = [
-        push(
-            shard,
-            out.at[me_dp, me_ctx],
-            zs.at[step - 1],
-            zr.at[step - 1],
-            {"ctx": place("ctx", step)},
+
+    def launch(item):
+        pl.when(item[1])(item[0].start)
+
+    def receive(item):
+        pl.when(item[2])(item[0].wait_recv)
+
+    def far_copy(owner, block, slot, far):
+        return pltpu.make_async_remote_copy(
+            src_ref=block,
+            dst_ref=out.at[me_dp, owner],
+            send_sem=xs.at[slot, far - 1],
+            recv_sem=xr.at[slot, far - 1],
+            device_id={"dp": place("dp", far)},
+            device_id_type=pl.DeviceIdType.MESH,
         )
-        for step in range(1, rows)
-    ]
+
     across = []
 
-    def send_across(step):
-        owner = place("ctx", -step)
-        block = shard if step == 0 else out.at[me_dp, owner]
+    def send_across(slot, owner, block, valid):
         for far in range(1, groups):
-            across.append(
-                push(
-                    block,
-                    out.at[me_dp, owner],
-                    xs.at[step, far - 1],
-                    xr.at[step, far - 1],
-                    {"dp": place("dp", far)},
-                )
-            )
-
-    send_across(0)
+            copy = far_copy(owner, block, slot, far)
+            pl.when(valid)(copy.start)
+            across.append((copy, valid))
+
+    def step_rest(step):
+        for side, item in enumerate(hops[step]):
+            receive(item)
+            send_across(1 + 2 * step + side, item[3], block_at(item[3]), item[2])
+
+    launch(kv_hops[0])
+    for item in hops[0]:
+        launch(item)
+    send_across(0, me_ctx, shard, me_ctx >= 0)
     all_kv[:, pl.ds(start, tokens), :] = local[...]
     out[me_dp, me_ctx] = shard[...]
-    for copy in kv_copies:
-        copy.wait()
+    for block in range(1, rows):
+
+        @pl.when(block > me_ctx)
+        def _(block=block):
+            later = all_kv.at[:, block * tokens : (block + 1) * tokens, :]
+            later[...] = jnp.zeros(later.shape, LOW)
+
+    for step in range(1, rows - 1):
+        receive(kv_hops[step - 1])
+        launch(kv_hops[step])
+        step_rest(step - 1)
+        for item in hops[step]:
+            launch(item)
+    receive(kv_hops[rows - 2])
     for one in range(batch):
         allowed = allowed_pairs(segment_row[one], segment_column[one])
         total[...] = jnp.zeros_like(total)
@@ -244,13 +279,11 @@
         lax.fori_loop(0, width // HD, one_head, 0)
         mixed[one] = total[...].astype(LOW)
         if one == 0:
-            for step in range(1, rows):
-                along[step - 1].wait_recv()
-                send_across(step)
-    for copy in across:
-        copy.wait_recv()
-    for copy in along + across:
-        copy.wait_send()
+            step_rest(rows - 2)
+    for copy, valid in across:
+        pl.when(valid)(copy.wait)
+    for item in kv_hops + [item for pair in hops for item in pair]:
+        pl.when(item[1])(item[0].wait_send)
 
 
 def attend(width, local, query, segment_row, segment_column, shard):
@@ -268,17 +301,18 @@
         in_specs=whole(5),
         out_specs=tuple(whole(3)),
         scratch_shapes=[pltpu.VMEM((tokens, value_width), F32)]
-        + [dma((rows - 1,))] * 4
-        + [dma((rows, groups - 1))] * 2,
+        + [dma((rows - 1,))] * 6
+        + [dma((2 * rows - 1, groups - 1))] * 2,
         compiler_params=params(2),
     )(local, query, segment_row, segment_column, shard)
 
 
 def attend_back_kernel(
     width, mixed_grad, query, all_kv, segment_row, segment_column, g0, g1, g2,
-    kv_grad, query_grad, value_sum, sum0, sum1, sum2,
+    down_part, middle, table,
+    kv_grad, query_grad, value_sum, sum0, sum1, sum2, result,
     total, parts, landing, dp0, dp1, dp2, pass0, pass1, pass2, ctx0, ctx1, ctx2,
-    ks, kr, xs, xr, zs, zr,
+    land_down, ks, kr, xs, xr, zs, zr, ds, dr,
 ):
     groups, rows = lax.axis_size("dp"), lax.axis_size("ctx")
     me_dp, me_ctx = lax.axis_index("dp"), lax.axis_index("ctx")
@@ -291,7 +325,8 @@
         (g2, sum2, dp2, pass2, ctx2),
     )
     order = list(range(1, rows)) + [0]
-    greet(("dp", "ctx"))
+    greet(("dp", "ctx", "tensor"))
+    down_copies = start_shares(down_part, land_down, ds, dr)
     across, along = {}, []
     for step in order:
         for at, (grads, _, land_dp, _, _) in enumerate(weights):
@@ -306,6 +341,30 @@
                 )
     value_sum[...] = jnp.zeros_like(value_sum)
     kv_copies = []
+
+    def pass_block(step):
+        owner = place("ctx", step)
+        for at, (grads, summed, land_dp, pass_on, land_ctx) in enumerate(weights):
+            for far in range(1, groups):
+                across[step, at, far].wait()
+            value = grads[me_dp, owner].astype(F32)
+            for far in range(1, groups):
+                value = value + land_dp[step, far - 1].astype(F32)
+            if step == 0:
+                summed[...] = value
+            else:
+                pass_on[step - 1] = value.astype(LOW)
+                along.append(
+                    push(
+                        pass_on.at[step - 1],
+                        land_ctx.at[step - 1],
+                        zs.at[at, step - 1],
+                        zr.at[at, step - 1],
+                        {"ctx": owner},
+                    )
+                )
+
+    pass_block(order[0])
     for one in range(batch):
         allowed = allowed_pairs(segment_row[one], segment_column[one])
         total[...] = jnp.zeros_like(total)
@@ -340,27 +399,14 @@
                 )
             )
         if one == 0:
-            for step in order:
-                owner = place("ctx", step)
-                for at, (grads, summed, land_dp, pass_on, land_ctx) in enumerate(weights):
-                    for far in range(1, groups):
-                        across[step, at, far].wait()
-                    value = grads[me_dp, owner].astype(F32)
-                    for far in range(1, groups):
-                        value = value + land_dp[step, far - 1].astype(F32)
-                    if step == 0:
-                        summed[...] = value
-                    else:
-                        pass_on[step - 1] = value.astype(LOW)
-                        along.append(
-                            push(
-                                pass_on.at[step - 1],
-                                land_ctx.at[step - 1],
-                                zs.at[at, step - 1],
-                                zr.at[at, step - 1],
-                                {"ctx": owner},
-                            )
-                        )
+            for step in order[1:]:
+                pass_block(step)
+    for copy in down_copies:
+        copy.wait()
+    share = middle.shape[1]
+    start = pl.multiple_of(lax.axis_index("tensor") * share, share)
+    value = sum_shares(down_part, land_down, start)
+    result[...] = (middle[...] + value + table[7:8][None]).astype(LOW)
     start = pl.multiple_of(me_ctx * tokens, tokens)
     for copy in kv_copies:
         copy.wait()
@@ -377,7 +423,9 @@
         summed[...] = value
 
 
-def attend_back(width, mixed_grad, query, all_kv, segment_row, segment_column, weight_grads):
+def attend_back(
+    width, mixed_grad, query, all_kv, segment_row, segment_column, weight_grads, down_part, middle, table
+):
     groups, rows = lax.axis_size("dp"), lax.axis_size("ctx")
     batch, tokens, key_width = query.shape
     length = rows * tokens
@@ -390,9 +438,10 @@
             jax.ShapeDtypeStruct(query.shape, F32),
             jax.ShapeDtypeStruct((8, 2 * width), F32),
         )
-        + tuple(jax.ShapeDtypeStruct(block, F32) for block in blocks),
-        in_specs=whole(8),
-        out_specs=tuple(whole(6)),
+        + tuple(jax.ShapeDtypeStruct(block, F32) for block in blocks)
+        + (jax.ShapeDtypeStruct(middle.shape, LOW),),
+        in_specs=whole(11),
+        out_specs=tuple(whole(7)),
         scratch_shapes=[
             pltpu.VMEM((length, 2 * width), F32),
             pltpu.VMEM((batch, length, 2 * width), LOW),
@@ -400,11 +449,16 @@
         ]
         + [pltpu.VMEM((rows, groups - 1) + block, LOW) for block in blocks]
         + [pltpu.VMEM((rows - 1,) + block, LOW) for block in blocks] * 2
+        + [pltpu.VMEM((lax.axis_size("tensor") - 1,) + middle.shape, LOW)]
         + [dma((batch, rows - 1))] * 2
         + [dma((3, rows, groups - 1))] * 2
-        + [dma((3, rows - 1))] * 2,
+        + [dma((3, rows - 1))] * 2
+        + [dma((lax.axis_size("tensor") - 1,))] * 2,
         compiler_params=params(3),
-    )(mixed_grad, query, all_kv, segment_row, segment_column, *weight_grads)
+    )(
+        mixed_grad, query, all_kv, segment_row, segment_column, *weight_grads,
+        down_part, middle, table,
+    )
 
 
 def start_shares(parts, landing, sends, receives):
@@ -431,16 +485,29 @@
     return total
 
 
-def spread_shares(out, start, share, sends, receives):
-    copies = []
-    for step in range(1, lax.axis_size("tensor")):
-        mine = out.at[:, pl.ds(start, share), :]
-        copies.append(
-            push(
-                mine, mine, sends.at[step - 1], receives.at[step - 1], {"tensor": place("tensor", step)}
-            )
-        )
-    return copies
+def spread_shares(out, start, share, sends, receives, meanwhile):
+    ways = lax.axis_size("tensor")
+    index = lax.axis_index("tensor")
+
+    def send(block, slot, peer):
+        rows = out.at[:, pl.ds(pl.multiple_of(block * share, share), share), :]
+        return push(rows, rows, sends.at[slot], receives.at[slot], {"tensor": peer})
+
+    if ways == 4:
+        far = lax.rem(index + 2, 4)
+        near = index + 1 - 2 * lax.rem(index, 2)
+        copies = [send(index, 0, far), send(index, 1, near)]
+        meanwhile()
+        copies[0].wait_recv()
+        copies.append(send(far, 2, near))
+    else:
+        copies = [send(index, step - 1, place("tensor", step)) for step in range(1, ways)]
+        meanwhile()
+        copies[0].wait_recv()
+    for copy in copies[1:]:
+        copy.wait_recv()
+    for copy in copies:
+        copy.wait_send()
 
 
 def forward_share_kernel(parts, inputs, table, out, middle, landing, s0, r0, s1, r1):
@@ -455,8 +522,7 @@
     middle[...] = values
     unit, scale = unit_norm(values)
     out[:, pl.ds(start, share), :] = (unit * table[5:6][None] + table[6:7][None]).astype(LOW)
-    for copy in spread_shares(out, start, share, s1, r1):
-        copy.wait()
+    spread_shares(out, start, share, s1, r1, lambda: None)
 
 
 def backward_share_kernel(parts, back, middle, table, out, grad, sums, landing, s0, r0, s1, r1):
@@ -472,12 +538,13 @@
     values = back_rows + norm_back(total, table[5:6][None], unit, scale)
     grad[...] = values
     out[:, pl.ds(start, share), :] = values.astype(LOW)
-    copies = spread_shares(out, start, share, s1, r1)
-    sums[...] = jnp.zeros_like(sums)
-    for row, term in enumerate((values, total * unit, total, back_rows)):
-        sums[row : row + 1] = jnp.sum(jnp.sum(term, axis=0), axis=0, keepdims=True)
-    for copy in copies:
-        copy.wait()
+
+    def add_rows():
+        sums[...] = jnp.zeros_like(sums)
+        for row, term in enumerate((values, total * unit, total, back_rows)):
+            sums[row : row + 1] = jnp.sum(jnp.sum(term, axis=0), axis=0, keepdims=True)
+
+    spread_shares(out, start, share, s1, r1, add_rows)
 
 
 def share_scratch(parts, copies):
@@ -520,14 +587,14 @@
 
 
 def final_kernel(
-    grads, first_part, down_part, inputs, middle, middle_grad, table, owned,
-    grad_sum, input_grad, result, vector_sum,
-    land_dp, pass_on, land_ctx, land_first, land_down, land_t, land_c, land_d,
-    xs, xr, zs, zr, fs, fr, ds, dr, ts, tr, cs, cr, es, er,
+    grads, first_part, inputs, middle_grad, table, owned,
+    grad_sum, input_grad, vector_sum,
+    land_dp, pass_on, land_ctx, land_first, land_t, land_c, land_d,
+    xs, xr, zs, zr, fs, fr, ts, tr, cs, cr, es, er,
 ):
     groups, rows = lax.axis_size("dp"), lax.axis_size("ctx")
     me_dp, me_ctx = lax.axis_index("dp"), lax.axis_index("ctx")
-    share = middle.shape[1]
+    share = middle_grad.shape[1]
     start = pl.multiple_of(lax.axis_index("tensor") * share, share)
     greet(("dp", "ctx", "tensor"))
     order = list(range(1, rows)) + [0]
@@ -543,7 +610,6 @@
                 {"dp": peer},
             )
     first_copies = start_shares(first_part, land_first, fs, fr)
-    down_copies = start_shares(down_part, land_down, ds, dr)
 
     along = []
     for step in order:
@@ -597,10 +663,6 @@
             summed = summed + land[step - 1]
         vector_sum[...] = summed
 
-    for copy in down_copies:
-        copy.wait()
-    total = sum_shares(down_part, land_down, start)
-    result[...] = (middle[...] + total + table[7:8][None]).astype(LOW)
     for copy in along:
         copy.wait()
     summed = grad_sum[...]
@@ -609,29 +671,27 @@
     grad_sum[...] = summed
 
 
-def finish(grads, first_part, down_part, inputs, middle, middle_grad, table, owned):
+def finish(grads, first_part, inputs, middle_grad, table, owned):
     groups, rows = lax.axis_size("dp"), lax.axis_size("ctx")
     ways = lax.axis_size("tensor")
     block = grads.shape[2:]
     dma = pltpu.SemaphoreType.DMA
-    land = pltpu.VMEM((ways - 1,) + middle.shape, LOW)
-    pairs = ((rows, groups - 1), (rows - 1,), (ways - 1,), (ways - 1,))
+    land = pltpu.VMEM((ways - 1,) + middle_grad.shape, LOW)
+    pairs = ((rows, groups - 1), (rows - 1,), (ways - 1,))
     pairs += ((ways - 1,), (rows - 1,), (groups - 1,))
     return pl.pallas_call(
         final_kernel,
         out_shape=(
             jax.ShapeDtypeStruct(block, F32),
-            jax.ShapeDtypeStruct(middle.shape, F32),
-            jax.ShapeDtypeStruct(middle.shape, LOW),
+            jax.ShapeDtypeStruct(middle_grad.shape, F32),
             jax.ShapeDtypeStruct(owned.shape, F32),
         ),
-        in_specs=whole(8),
-        out_specs=tuple(whole(4)),
+        in_specs=whole(6),
+        out_specs=tuple(whole(3)),
         scratch_shapes=[
             pltpu.VMEM((rows, groups - 1) + block, LOW),
             pltpu.VMEM((rows - 1,) + block, LOW),
             pltpu.VMEM((rows - 1,) + block, LOW),
-            land,
             land,
             pltpu.VMEM((ways - 1,) + owned.shape, F32),
             pltpu.VMEM((rows - 1,) + owned.shape, F32),
@@ -639,7 +699,7 @@
         ]
         + [dma(shape) for shape in pairs for _ in range(2)],
         compiler_params=params(6),
-    )(grads, first_part, down_part, inputs, middle, middle_grad, table, owned)
+    )(grads, first_part, inputs, middle_grad, table, owned)
 
 
 def on_device(
@@ -731,8 +791,9 @@
     weight_grads = [
         grads.astype(LOW).reshape(blocks + (-1,)) for grads in (grad_up, grad_down, grad_out)
     ]
-    kv_grad, query_grad, value_sum, up_sum, down_sum, out_sum = attend_back(
-        width, mixed_grad, query, all_kv, segment_row, segment_column, weight_grads
+    kv_grad, query_grad, value_sum, up_sum, down_sum, out_sum, result = attend_back(
+        width, mixed_grad, query, all_kv, segment_row, segment_column, weight_grads,
+        down_part, middle, table,
     )
     query_grad = query_grad[:, :, :width]
     stacked = jnp.concatenate([query_grad.astype(LOW), kv_grad], axis=2).reshape(
@@ -754,8 +815,8 @@
         owned, jnp.sum(hidden_grad, axis=0), (8 * model + tensor_index * units,)
     ).reshape(small.shape[0], model)
 
-    grad_sum, input_grad, result, vector_sum = finish(
-        grads, first_part, down_part, hidden_in, middle, middle_grad, table, owned
+    grad_sum, input_grad, vector_sum = finish(
+        grads, first_part, hidden_in, middle_grad, table, owned
     )
     grad_vectors = lax.dynamic_slice_in_dim(
         vector_sum[:table_rows],

time: 299 us -> 263 us (0.88)
  Pallas kernels: 249 us -> 218 us
  local copies, waits for them, and re-layouts: 21.5 us -> 18.5 us
    pallas_call x1, Pallas kernels: 75 us -> 42.4 us  [attend(): pl.pallas_call(functools.partial(attend_kernel, width), out_shape=(jax.Sh...]
    pallas_call x1, Pallas kernels: 76.5 us -> 88.3 us  [attend_back(): pl.pallas_call(functools.partial(attend_back_kernel, width), out_shape=(j...]
    pallas_call x1, Pallas kernels: 34.6 us -> 29.1 us  [finish(): pl.pallas_call(final_kernel, out_shape=(jax.ShapeDtypeStruct(block, F32),...]
    unnamed x80 -> x88, local copies, waits for them, and re-layouts: 15.4 us -> 12.6 us
where the time goes in v4:
time: 263 us
  Pallas kernels  218 us (83%)
  local copies, waits for them, and re-layouts  18.5 us (7%)
  matrix products  15.4 us (6%)
  other arithmetic  9.27 us (4%)
    pallas_call x1, Pallas kernels, attend_back(): pl.pallas_call(functools.partial(attend_back_kernel, width), out_shape=(j...  88.3 us
    pallas_call x1, Pallas kernels, attend(): pl.pallas_call(functools.partial(attend_kernel, width), out_shape=(jax.Sh...  42.4 us
    pallas_call x1, Pallas kernels, finish(): pl.pallas_call(final_kernel, out_shape=(jax.ShapeDtypeStruct(block, F32),...  29.1 us
    pallas_call x1, Pallas kernels, gather_weights(): pl.pallas_call(weights_kernel, out_shape=(jax.ShapeDtypeStruct((groups, r...  22.2 us
    pallas_call x1, Pallas kernels, backward_share(): pl.pallas_call(backward_share_kernel, out_shape=(jax.ShapeDtypeStruct(par...  18 us
    pallas_call x1, Pallas kernels, forward_share(): pl.pallas_call(forward_share_kernel, out_shape=(jax.ShapeDtypeStruct(part...  18 us
    dot_general x12, matrix products, dot(): lax.dot_general(left, right, (((left_dim,), (right_dim,)), ((), ())), pre...  15.4 us
    unnamed x88, local copies, waits for them, and re-layouts  12.6 us

profile of v4, /device:TPU:0, one launch (start us, length us, event | category | flops | bytes accessed | tf_op | source)
XLA Modules:
  0.0 262.5 jit_solution(7614150456714784471)
XLA Ops:
  0.7 0.8 dynamic-slice_bitcast_fusion
  1.5 1.4 convert_reduce_fusion
  2.9 1.5 fusion.2
  6.5 22.2 %shard_map.305 = (bf16[2,4,96,576]{3,2,1,0:T(8,128)(2,1)S(1)}, bf16[2,4,16,128]{3,2,1,0:T(8,128)(2,1)S(1)}) custom-call(bf16[96,576]{1,0:T(8,128)(2,1)S(1)} %pad_maximum_fusion.4.shard, bf16[16,128]{1,0:T(8,128)(2,1)S(1)} %pad.12.small), custom_call_target="tpu_custom_call" | custom-call | tf_op jit(solution)/shard_map/pallas_call | solution.py:147
  31.3 42.4 %shard_map.306 = (bf16[2,1024,384]{2,1,0:T(8,128)(2,1)S(1)}, bf16[2,256,256]{2,1,0:T(8,128)(2,1)S(1)}, bf16[2,4,96,1728]{3,2,1,0:T(8,128)(2,1)S(1)}) custom-call(bf16[2,256,384]{2,1,0:T(8,128)(2,1)S(1)} %pad_maximum_fusion.1.local, bf16[2,256,256]{2,1,0:T(8,128)(2,1)S(1)} %pad.13.query, s32[2,1,1024]{2,1,0:T(1,128)S(1)} %broadcast_in_dim.6.segment_row, ...), custom_call_target="tpu_custom_call" | custom-call | tf_op jit(solution)/shard_map/pallas_call | solution.py:294
  73.8 1.2 copy-done.1
  75.5 18.0 %shard_map.307 = (bf16[2,256,768]{2,1,0:T(8,128)(2,1)S(1)}, f32[2,64,768]{2,1,0:T(8,128)S(1)}) custom-call(bf16[2,256,768]{2,1,0:T(8,128)(2,1)S(1)} %bitcast.96, bf16[2,256,768]{2,1,0:T(8,128)(2,1)S(1)} %copy-done, f32[16,768]{1,0:T(8,128)S(1)} %convert_element_type.75.table), custom_call_target="tpu_custom_call" | custom-call | tf_op jit(solution)/shard_map/pallas_call | solution.py:561
  93.5 0.8 convolution_add_fusion
  94.3 2.0 convolution_convert_fusion.2
  96.3 2.1 fusion.42
  98.4 2.0 convolution_convert_fusion
  100.4 1.8 convolution_convert_fusion.1
  102.3 0.8 convolution_convert_fusion.3
  103.1 18.0 %shard_map.308 = (bf16[2,256,768]{2,1,0:T(8,128)(2,1)S(1)}, f32[2,64,768]{2,1,0:T(8,128)S(1)}, f32[8,768]{1,0:T(8,128)S(1)}) custom-call(bf16[2,256,768]{2,1,0:T(8,128)(2,1)S(1)} %bitcast.106, bf16[2,256,768]{2,1,0:T(8,128)(2,1)S(1)} %copy-done.6, f32[2,64,768]{2,1,0:T(8,128)S(1)} %get-tuple-element.42.middle, f32[16,768]{1,0:T(8,128)S(1)} %convert_element_type.75.table), custom_call_target="tpu_custom_call" | custom-call | tf_op jit(solution)/shard_map/pallas_call | solution.py:575
  123.9 1.3 copy-done.2
  125.2 1.1 copy-done.5
  126.3 88.3 %shard_map.309 = (bf16[2,256,384]{2,1,0:T(8,128)(2,1)S(1)}, f32[2,256,256]{2,1,0:T(8,128)S(1)}, f32[8,384]{1,0:T(8,128)S(1)}, f32[96,768]{1,0:T(8,128)S(1)}, f32...) custom-call(bf16[2,256,256]{2,1,0:T(8,128)(2,1)S(1)} %pad.14.mixed_grad, ...), custom_call_target="tpu_custom_call" | custom-call | tf_op jit(solution)/shard_map/pallas_call | solution.py:434
  218.6 3.1 %bitcast_convert_fusion = bf16[768,576]{0,1:T(8,128)(2,1)} fusion(bf16[2,256,768]{2,1,0:T(8,128)(2,1)} %copy-done.17, bf16[2,256,384]{2,1,0:T(8,128)(2,1)S(1)} %get-tuple-element.47, bf16[2,256,192]{2,1,0:T(8,128)(2,1)S(1)} %slice.151), kind=kOutput, calls=%fused_computation.6 | convolution fusion | flops 454606848 | bytes 2260992 | tf_op jit(solution)/shard_map/dot_general | solution.py:29
  222.0 0.8 convolution_convert_fusion.4
  222.8 1.6 copy.63
  224.5 29.1 %shard_map.310 = (f32[96,576]{1,0:T(8,128)S(1)}, f32[2,64,768]{2,1,0:T(8,128)S(1)}, f32[16,768]{1,0:T(8,128)S(1)}) custom-call(bf16[2,4,96,576]{3,2,1,0:T(8,128)(2,1)S(1)} %bitcast.95, bf16[2,256,768]{2,1,0:T(8,128)(2,1)S(1)} %bitcast.105, bf16[2,256,768]{2,1,0:T(8,128)(2,1)S(1)} %copy-done, f32[2,64,768]{2,1,0:T(8,128)S(1)} %copy-done.8, ...), custom_call_target="tpu_custom_call" | custom-call | tf_op jit(solution)/shard_map/pallas_call | solution.py:682
  256.7 2.3 multiply_subtract_fusion.2
  259.0 1.0 multiply_subtract_fusion.1
  260.0 1.0 multiply_subtract_fusion
  (140 shorter events, 16.6 us)
Async XLA Ops:
  0.7 3.8 %copy-start.35 = (f32[12,96]{1,0:T(8,128)S(1)}, f32[12,96]{1,0:T(8,128)}, u32[]{:S(2)}) copy-start(f32[12,96]{1,0:T(8,128)} %param.33) | copy-start | bytes 13828
  0.7 5.4 %copy-start.18 = (f32[3,96,192]{2,1,0:T(8,128)S(1)}, f32[3,96,192]{2,1,0:T(8,128)}, u32[]{:S(2)}) copy-start(f32[3,96,192]{2,1,0:T(8,128)} %param.21) | copy-start | bytes 663556
  0.7 3.8 %copy-start.36 = (s32[2,1024]{1,0:T(2,128)S(1)}, s32[2,1024]{1,0:T(2,128)}, u32[]{:S(2)}) copy-start(s32[2,1024]{1,0:T(2,128)} %param.20) | copy-start | bytes 24580
  0.7 4.7 %copy-start.33 = (f32[192,96]{1,0:T(8,128)S(1)}, f32[192,96]{1,0:T(8,128)}, u32[]{:S(2)}) copy-start(f32[192,96]{1,0:T(8,128)} %param.26) | copy-start | bytes 221188
  0.7 3.9 %copy-start.32 = (f32[192,96]{1,0:T(8,128)S(1)}, f32[192,96]{1,0:T(8,128)}, u32[]{:S(2)}) copy-start(f32[192,96]{1,0:T(8,128)} %param.25) | copy-start | bytes 221188
  0.7 3.8 %copy-start.31 = (f32[192,96]{1,0:T(8,128)S(1)}, f32[192,96]{1,0:T(8,128)}, u32[]{:S(2)}) copy-start(f32[192,96]{1,0:T(8,128)} %param.24) | copy-start | bytes 221188
  1.5 4.8 %copy-start.19 = (f32[96,768]{1,0:T(8,128)S(1)}, f32[96,768]{1,0:T(8,128)}, u32[]{:S(2)}) copy-start(f32[96,768]{1,0:T(8,128)} %param.27) | copy-start | bytes 884740
  2.9 3.4 %copy-start.21 = (f32[768,96]{0,1:T(8,128)S(1)}, f32[768,96]{0,1:T(8,128)}, u32[]{:S(2)}) copy-start(f32[768,96]{0,1:T(8,128)} %param.30) | copy-start | bytes 884740
  6.1 23.2 %copy-start = (bf16[2,256,768]{2,1,0:T(8,128)(2,1)S(1)}, bf16[2,256,768]{2,1,0:T(8,128)(2,1)}, u32[]{:S(2)}) copy-start(bf16[2,256,768]{2,1,0:T(8,128)(2,1)} %inputs.3) | copy-start | bytes 2359300
  126.3 90.4 %copy-start.24 = (f32[192,96]{0,1:T(8,128)S(1)}, f32[192,96]{0,1:T(8,128)}, u32[]{:S(2)}) copy-start(f32[192,96]{0,1:T(8,128)} %copy-done.23) | copy-start | bytes 221188
  126.3 90.4 %copy-start.25 = (f32[192,96]{0,1:T(8,128)S(1)}, f32[192,96]{0,1:T(8,128)}, u32[]{:S(2)}) copy-start(f32[192,96]{0,1:T(8,128)} %copy.64) | copy-start | bytes 221188
  126.3 90.4 %copy-start.26 = (f32[192,96]{0,1:T(8,128)S(1)}, f32[192,96]{0,1:T(8,128)}, u32[]{:S(2)}) copy-start(f32[192,96]{0,1:T(8,128)} %copy.65) | copy-start | bytes 221188
  218.6 3.4 %copy-start.4 = (bf16[2,4,96,576]{3,2,1,0:T(8,128)(2,1)S(1)}, bf16[2,4,96,576]{3,2,1,0:T(8,128)(2,1)}, u32[]{:S(2)}) copy-start(bf16[2,4,96,576]{3,2,1,0:T(8,128)(2,1)} %copy-done.3) | copy-start | bytes 2654212
  224.4 29.9 %copy-start.37 = (f32[12,96]{1,0:T(8,128)S(1)}, f32[12,96]{1,0:T(8,128)}, u32[]{:S(2)}) copy-start(f32[12,96]{1,0:T(8,128)} %param.34) | copy-start | bytes 13828
  224.4 29.9 %copy-start.38 = (f32[12,96]{1,0:T(8,128)S(1)}, f32[12,96]{1,0:T(8,128)}, u32[]{:S(2)}) copy-start(f32[12,96]{1,0:T(8,128)} %param.35) | copy-start | bytes 13828
  254.3 4.6 %copy-start.14 = (f32[96,768]{1,0:T(8,128)S(1)}, f32[96,768]{1,0:T(8,128)}, u32[]{:S(2)}) copy-start(f32[96,768]{1,0:T(8,128)} %copy-done.13) | copy-start | bytes 884740
  254.3 4.6 %copy-start.20 = (f32[96,768]{1,0:T(8,128)S(1)}, f32[96,768]{1,0:T(8,128)}, u32[]{:S(2)}) copy-start(f32[96,768]{1,0:T(8,128)} %param.27) | copy-start | bytes 884740
  254.3 4.6 %copy-start.27 = (f32[96,768]{1,0:T(8,128)S(1)}, f32[96,768]{1,0:T(8,128)}, u32[]{:S(2)}) copy-start(f32[96,768]{1,0:T(8,128)} %param.28) | copy-start | bytes 884740
  254.3 4.6 %copy-start.28 = (f32[96,768]{1,0:T(8,128)S(1)}, f32[96,768]{1,0:T(8,128)}, u32[]{:S(2)}) copy-start(f32[96,768]{1,0:T(8,128)} %param.29) | copy-start | bytes 884740
  256.6 3.4 %copy-start.12 = (f32[96,768]{1,0:T(8,128)S(1)}, f32[96,768]{1,0:T(8,128)}, u32[]{:S(2)}) copy-start(f32[96,768]{1,0:T(8,128)} %copy-done.11) | copy-start | bytes 884740
  256.6 3.4 %copy-start.22 = (f32[768,96]{0,1:T(8,128)S(1)}, f32[768,96]{0,1:T(8,128)}, u32[]{:S(2)}) copy-start(f32[768,96]{0,1:T(8,128)} %param.30) | copy-start | bytes 884740
  256.6 3.4 %copy-start.29 = (f32[768,96]{0,1:T(8,128)S(1)}, f32[768,96]{0,1:T(8,128)}, u32[]{:S(2)}) copy-start(f32[768,96]{0,1:T(8,128)} %param.31) | copy-start | bytes 884740
  256.7 3.4 %copy-start.30 = (f32[768,96]{0,1:T(8,128)S(1)}, f32[768,96]{0,1:T(8,128)}, u32[]{:S(2)}) copy-start(f32[768,96]{0,1:T(8,128)} %param.32) | copy-start | bytes 884740
  259.0 2.1 copy-start.16
  (16 other events, 19.1 us)
